TPU v7x, 32 devices: a whole 2x2x4 slice. The times are simulated.
32 devices in a mesh: grp: 2 (over x), wave: 16 (over z, y, core).
Axes of the slice: x: 2, y: 2, z: 4, core: 2. Of those that a mesh axis runs over, the one named last changes fastest.
Arguments:
- spectral: bfloat16 [640, 641, 256], P(('grp', 'wave')), parts along dimension 0, may hold values from -0.23925781 to 0.23925781
- legendre: bfloat16 [320, 641, 320], P('wave'), may hold values from -0.25 to 0.25
- pair_low: int32 [320], replicated, may hold values from 0 to 319, each once
- routes: int32 [102400, 1], P(('grp', 'wave')), parts along dimension 0, may hold values from 0 to 15; in each aligned block of 3200 rows (0 to 3199, 3200 to 6399, ...) at most 400 rows name the same one
- w_in: bfloat16 [16, 128, 1024], P('wave'), may hold values from -0.5 to 0.5
- w_mid: bfloat16 [16, 1024, 1024], P('wave'), may hold values from -0.1875 to 0.1875
- w_out: bfloat16 [16, 1024, 128], P('wave'), may hold values from -1.5 to 1.5
Outputs:
- tendency: bfloat16 [640, 641, 256], P(('grp', 'wave')), parts along dimension 0
There are 2 independent parts, one for each index of `grp`. A program takes and returns all parts, laid end to end along the dimension named above; an argument that names none is the same for every part. Nothing has to cross between parts.
Inputs may be any that keep to these rules, and one draw needn't show every extreme that they name: `routes`: among the columns of one device (each aligned block of 3200 columns) at most 400 name the same network, a bound that some block reaches of them.
All inputs are finite; a program needn't handle non-finite values.
Results may differ from a plain program's by a relative error of at most 0.01.
Values may be sent and summed in bfloat16 or wider, within the bound.
No kernel may reach another device: no remote copies, remote signals or barrier semaphores. Data moves between devices by JAX's collectives and lax.ppermute only.
A program may use at most 192 MiB of HBM per device.

v0:
```python
import math

import jax
import jax.numpy as jnp
from jax import lax
from jax.sharding import PartitionSpec as P

NLON = 1280
FIELDS = 4


def slot_waves(pair_low, wave_total):
    return jnp.stack([pair_low, wave_total - 1 - pair_low], axis=1).reshape(-1)


def side_masks(pair_low, wave_total):
    degree = jnp.arange(wave_total + 1, dtype=jnp.int32)
    lower_side = degree[None, :] < (wave_total - pair_low)[:, None]
    return jnp.stack([lower_side, jnp.logical_not(lower_side)], axis=1)


def fourier_table(wavenums, points, inverse):
    longitude = jnp.arange(points, dtype=jnp.int32)
    phases = wavenums[:, None] * longitude[None, :] % points
    angles = phases.astype(jnp.float32) * jnp.float32(2.0 * math.pi / points)
    if inverse:
        factor = jnp.where(wavenums == 0, jnp.float32(1.0), jnp.float32(2.0))[:, None]
    else:
        factor = jnp.full((wavenums.shape[0], 1), 1.0 / math.sqrt(points), jnp.float32)
    return jnp.stack([factor * jnp.cos(angles), -factor * jnp.sin(angles)], axis=1).astype(
        jnp.bfloat16
    )


def forcing(grid_fields):
    flattened = grid_fields.reshape(FIELDS, -1)
    return (flattened * jnp.roll(flattened, -1, axis=0)).reshape(grid_fields.shape)


def coarse_columns(grid_fields):
    feat_width = grid_fields.shape[0]
    lat_rows = grid_fields.shape[1]
    lon_count = grid_fields.shape[2]
    blocks = grid_fields.reshape(feat_width, lat_rows // 2, 2, lon_count // 4, 4).mean(axis=(2, 4))
    return blocks.reshape(feat_width, -1).T.astype(jnp.bfloat16)


def spread_back(values, lat_rows):
    feat_width = values.shape[1]
    coarse = values.astype(jnp.float32).T.reshape(feat_width, lat_rows // 2, -1)
    before = jnp.roll(coarse, 1, axis=2)
    following = jnp.roll(coarse, -1, axis=2)
    pieces = [
        0.375 * before + 0.625 * coarse,
        0.125 * before + 0.875 * coarse,
        0.875 * coarse + 0.125 * following,
        0.625 * coarse + 0.375 * following,
    ]
    fine_grid = jnp.stack(pieces, axis=3).reshape(feat_width, lat_rows // 2, -1)
    return jnp.repeat(fine_grid, 2, axis=1)


def slot_positions(regimes, experts_total):
    onehot = (regimes[:, :, None] == jnp.arange(experts_total, dtype=jnp.int32)).astype(jnp.int32)
    ranking = jnp.cumsum(onehot, axis=1) - 1
    return jnp.sum(ranking * onehot, axis=2)


def network(columns, weight_in, weight_mid, weight_out):
    hidden = jax.nn.silu(jnp.dot(columns, weight_in, preferred_element_type=jnp.float32)).astype(
        jnp.bfloat16
    )
    deeper = jax.nn.silu(jnp.dot(hidden, weight_mid, preferred_element_type=jnp.float32)).astype(
        jnp.bfloat16
    )
    return jnp.dot(deeper, weight_out, preferred_element_type=jnp.float32).astype(jnp.bfloat16)


def masked_inverse(spectral, legendre, side_mask):
    masked = jnp.where(side_mask[:, :, :, None], spectral[:, None], jnp.zeros((), jnp.bfloat16))
    return jnp.einsum("psjc,pjl->pscl", masked, legendre, preferred_element_type=jnp.float32)


def masked_forward(legendre, coeffs, side_mask):
    both_sides = jnp.einsum(
        "pjl,pskrl->psjkr", legendre, coeffs, preferred_element_type=jnp.float32
    )
    return jnp.sum(jnp.where(side_mask[:, :, :, None, None], both_sides, 0.0), axis=1)


def on_device(spectral, legendre, pair_low, routes, w_in, w_mid, w_out):
    pair_count = spectral.shape[0]
    degrees = spectral.shape[1]
    channels = spectral.shape[2]
    feat_width = channels // 2
    lat_total = legendre.shape[2]
    wave_total = degrees - 1
    devices = lax.axis_size("wave")
    local_low = lax.dynamic_slice_in_dim(pair_low, lax.axis_index("wave") * pair_count, pair_count)
    side_mask = side_masks(local_low, wave_total)
    inverse_out = masked_inverse(spectral, legendre, side_mask)
    fourier_in = inverse_out.astype(jnp.bfloat16).reshape(2 * pair_count, feat_width, 2, lat_total)
    wavenums = slot_waves(pair_low, wave_total)
    inverse_table = fourier_table(wavenums, NLON, True)
    grid_fields = jnp.einsum(
        "qkra,qrl->kal",
        lax.all_to_all(fourier_in, "wave", split_axis=3, concat_axis=0, tiled=True),
        inverse_table,
        preferred_element_type=jnp.float32,
    )
    lat_rows = grid_fields.shape[1]
    forced = forcing(grid_fields)
    columns = coarse_columns(grid_fields)
    regimes = routes[:, 0].reshape(1, -1)
    positions = slot_positions(regimes, devices)[0]
    regime_row = regimes[0]
    capacity = 2 * columns.shape[0] // devices
    outgoing = (
        jnp.zeros((devices, capacity, feat_width), jnp.bfloat16)
        .at[regime_row, positions]
        .set(columns)
    )
    arrived = lax.all_to_all(outgoing, "wave", split_axis=0, concat_axis=0, tiled=True)
    answers = network(arrived.reshape(-1, feat_width), w_in[0], w_mid[0], w_out[0]).reshape(
        arrived.shape
    )
    incoming = lax.all_to_all(answers, "wave", split_axis=0, concat_axis=0, tiled=True)
    returned = incoming[regime_row, positions]
    correction = spread_back(returned, lat_rows)
    tendency_grid = (forced + correction).astype(jnp.bfloat16)
    forward_table = fourier_table(wavenums, NLON, False)
    fourier_out = jnp.einsum(
        "fal,qrl->qfra", tendency_grid, forward_table, preferred_element_type=jnp.float32
    ).astype(jnp.bfloat16)
    received = lax.all_to_all(fourier_out, "wave", split_axis=0, concat_axis=3, tiled=True)
    coeffs = received.reshape(pair_count, 2, received.shape[1], 2, received.shape[3])
    result = masked_forward(legendre, coeffs, side_mask)
    spectral_out = result.astype(jnp.bfloat16)
    return spectral_out.reshape(pair_count, degrees, channels)


def solution(mesh):
    placed = (
        P(("grp", "wave"), None, None),
        P("wave", None, None),
        P(),
        P(("grp", "wave"), None),
        P("wave", None, None),
        P("wave", None, None),
        P("wave", None, None),
    )
    return jax.shard_map(
        on_device,
        mesh=mesh,
        in_specs=placed,
        out_specs=P(("grp", "wave"), None, None),
        check_vma=False,
    )
```

profile of v0, /device:TPU:13, one launch (start us, length us, event | category | flops | bytes accessed | tf_op | source)
XLA Modules:
  0.0 717.0 jit_solution(5438922527559547650)
XLA Ops:
  1.9 10.8 %fusion.11 = bf16[20,2,256,320]{2,3,1,0:T(8,128)(2,1)} fusion(bf16[20,641,320]{1,2,0:T(8,128)(2,1)} %param.8, pred[20,2,641]{2,1,0:T(4,128)(4,1)S(1)} %pad_add_fusion, bf16[20,641,256]{2,1,0:T(8,128)(2,1)} %param.7), kind=kOutput, calls=%fused_computation.19 | convolution fusion | flops 4210698240 | bytes 21347880 | tf_op jit(solution)/shard_map/psjc,pjl->pscl/dot_general | solution.py:81
  12.7 9.8 %copy.121 = bf16[20,2,256,320]{3,2,1,0:T(8,128)(2,1)} copy(bf16[20,2,256,320]{2,3,1,0:T(8,128)(2,1)} %fusion.11) | data formatting | bytes 13107200 | tf_op jit(solution)/shard_map/convert_element_type | solution.py:102
  22.5 16.4 %reshape.601 = bf16[40,128,2,320]{3,2,1,0:T(2,128)(2,1)} reshape(bf16[20,2,256,320]{3,2,1,0:T(8,128)(2,1)} %copy.121) | data formatting | bytes 13107200 | tf_op jit(solution)/shard_map/reshape | solution.py:102
  38.8 14.4 %copy.122 = bf16[40,128,2,320]{1,0,2,3:T(8,128)(2,1)} copy(bf16[40,128,2,320]{3,2,1,0:T(2,128)(2,1)} %reshape.601) | data formatting | bytes 13107200 | tf_op jit(solution)/shard_map/reshape | solution.py:102
  67.2 16.9 %multiply_convert_fusion.9 = (bf16[640,1,1280]{2,0,1:T(8,128)(2,1)}, bf16[640,1,1280]{2,0,1:T(8,128)(2,1)}, bf16[640,1,1280]{2,0,1:T(8,128)(2,1)}, bf16[640,1,1280]{2,0,1:T(8,128)(2,1)}) fusion(s32[640]{0:T(1024)S(1)} %mul.201, f32[640]{0:T(1024)S(1)} %get-tuple-element.23, f32[640]{0:T(1024)S(1)} %get-tuple-element.22), kind=kLoop, calls=%fused_computation.40 | loop fusion | flops 13926400 | bytes 6561280 | tf_op jit(solution)/shard_map/convert.5
  84.1 119.0 %all-to-all-done = bf16[40,128,2,320]{1,0,2,3:T(8,128)(2,1)} async-done(((bf16[40,128,2,320]{1,0,2,3:T(8,128)(2,1)}), bf16[40,128,2,320]{1,0,2,3:T(8,128)(2,1)}, u32[]{:S(2)}, u32[]{:S(2)}) %all-to-all-start) | async-done | bytes 6553632 | tf_op jit(solution)/shard_map/all_to_all | solution.py:107
  208.0 11.8 %convolution_bitcast_fusion = f32[128,20,1280]{2,0,1:T(8,128)} fusion(bf16[640,128,2,20]{1,0,3,2:T(8,128)(2,1)S(1)} %bitcast.126, bf16[640,1,1280]{2,0,1:T(8,128)(2,1)S(1)} %copy-done.5, bf16[640,1,1280]{2,0,1:T(8,128)(2,1)S(1)} %copy-done.6), kind=kOutput, calls=%fused_computation.18 | convolution fusion | flops 8390246400 | bytes 22937600 | tf_op jit(solution)/shard_map/qkra,qrl->kal/dot_general | solution.py:105
  219.7 13.9 %copy.129 = f32[128,20,1280]{0,2,1:T(8,128)} copy(f32[128,20,1280]{2,0,1:T(8,128)} %convolution_bitcast_fusion) | data formatting | bytes 26214400 | tf_op jit(solution)/shard_map/qkra,qrl->kal/dot_general | solution.py:105
  233.7 18.5 %reduce_sum.31 = f32[128,10,320]{0,2,1:T(8,128)} reduce(f32[128,10,2,320,4]{0,4,3,2,1:T(4,128)} %bitcast.116, f32[]{:T(128)} %constant.64.clone.1), dimensions={2,4}, to_apply=%region_3.4 | reduce | flops 2867200 | bytes 14745604 | tf_op jit(solution)/shard_map/reduce_sum | solution.py:44
  253.7 14.9 %scatter_custom_fusion = bf16[6400,128]{1,0:T(8,128)(2,1)} fusion(s32[3200]{0:T(1024)S(1)} %broadcast_select_fusion, bf16[3200,128]{1,0:T(8,128)(2,1)S(1)} %bitcast.130, bf16[]{:T(256)} %constant.19.clone.1), kind=kCustom, calls=%fused_computation.63 | custom fusion | bytes 1638402
  282.6 10.1 %copy.126 = f32[96,20,1280]{2,1,0:T(8,128)} copy(f32[96,20,1280]{2,0,1:T(8,128)S(1)} %slice.48) | data formatting | bytes 19660800 | tf_op jit(solution)/shard_map/jit(_roll_static)/slice | solution.py:37
  292.7 14.8 %slice.37 = f32[3,819200]{1,0:T(4,128)} reshape(f32[96,20,1280]{2,1,0:T(8,128)} %copy.126) | data formatting | bytes 19660800 | tf_op jit(solution)/shard_map/jit(_roll_static)/slice | solution.py:37
  320.4 24.3 %fusion.4 = f32[6400,1024]{1,0:T(8,128)} fusion(bf16[6400,128]{1,0:T(8,128)(2,1)} %bitcast.18, bf16[1,1024,1024]{2,1,0:T(8,128)(2,1)S(1)} %copy-done, bf16[1,128,1024]{2,1,0:T(8,128)(2,1)S(1)} %copy-done.13), kind=kOutput, calls=%fused_computation.12 | convolution fusion | flops 15132262400 | bytes 30212096 | tf_op jit(solution)/shard_map/dot_general | solution.py:73
  344.7 12.9 %fusion.10 = bf16[6400,128]{1,0:T(8,128)(2,1)} fusion(f32[6400,1024]{1,0:T(8,128)} %fusion.4, bf16[1,1024,128]{2,1,0:T(8,128)(2,1)S(1)} %copy-done.14), kind=kOutput, calls=%fused_computation.17 | convolution fusion | flops 1711308800 | bytes 28114944 | tf_op jit(solution)/shard_map/dot_general | solution.py:76
  363.6 15.7 %pad_maximum_fusion = f32[4,819200]{1,0:T(4,128)} fusion(f32[1,819200]{1,0:T(1,128)} %slice.39, f32[3,819200]{1,0:T(4,128)} %slice.37), kind=kLoop, calls=%fused_computation.8 | loop fusion | flops 3276800 | bytes 26214400 | tf_op jit(solution)/shard_map/jit(_roll_static)/concatenate | solution.py:37
  379.4 26.9 %concatenate.55 = f32[128,20,1280]{2,1,0:T(8,128)} reshape(f32[4,819200]{1,0:T(4,128)} %pad_maximum_fusion) | data formatting | bytes 26214400 | tf_op jit(solution)/shard_map/jit(_roll_static)/concatenate | solution.py:37
  406.4 17.6 %gather_fusion = bf16[3200,128]{1,0:T(8,128)(2,1)S(1)} fusion(bf16[16,400,128]{2,1,0:T(8,128)(2,1)S(1)} %all-to-all-done.2, s32[3200]{0:T(1024)S(1)} %copy-done.2), kind=kCustom, calls=%fused_computation | custom fusion | bytes 1664000 | tf_op jit(solution)/shard_map/gather | solution.py:128
  441.2 14.1 %fusion.3 = bf16[128,20,1280]{2,0,1:T(8,128)(2,1)S(1)} fusion(f32[128,20,1280]{2,0,1:T(8,128)} %convolution_bitcast_fusion, f32[128,20,1280]{2,1,0:T(8,128)} %concatenate.55, f32[128,10,1280]{2,0,1:T(8,128)} %copy.138), kind=kLoop, calls=%fused_computation.10 | loop fusion | flops 9830400 | bytes 39321600 | tf_op jit(solution)/shard_map/convert_element_type | solution.py:130
  464.6 38.3 %copy.139 = bf16[640,128,2,20]{1,2,3,0:T(2,128)(2,1)S(1)} copy(bf16[640,128,2,20]{1,0,3,2:T(8,128)(2,1)S(1)} %convert_bitcast_fusion.1) | data formatting | bytes 13107200 | tf_op jit(solution)/shard_map/convert_element_type | solution.py:134
  502.9 148.6 %all_to_all.43 = bf16[640,128,2,20]{1,2,3,0:T(2,128)(2,1)S(1)} all-to-all(bf16[640,128,2,20]{1,2,3,0:T(2,128)(2,1)S(1)} %copy.139), channel_id=1, replica_groups=mesh['grp'=2,'wave'=16] {'wave'}, dimensions={0} | all-to-all | bytes 13107200 | tf_op jit(solution)/shard_map/all_to_all | solution.py:135
  654.2 15.6 %select_reduce_fusion = bf16[20,128,2,641]{1,3,2,0:T(8,128)(2,1)} fusion(pred[20,2,641]{2,1,0:T(4,128)(4,1)S(1)} %copy-done.8, bf16[20,641,320]{1,2,0:T(8,128)(2,1)} %param.8, bf16[20,2,128,2,320]{2,1,0,4,3:T(2,128)(2,1)S(1)} %bitcast.127), kind=kOutput, calls=%fused_computation.2 | convolution fusion | flops 4210703360 | bytes 21347880 | tf_op jit(solution)/shard_map/pjl,pskrl->psjkr/dot_general | solution.py:85
  669.8 19.9 %copy.143 = bf16[20,641,128,2]{1,3,2,0:T(2,128)(2,1)} copy(bf16[20,641,128,2]{2,1,3,0:T(8,128)(2,1)} %bitcast.125) | data formatting | bytes 13127680 | tf_op jit(solution)/shard_map/convert_element_type | solution.py:138
  689.8 16.9 %convert_element_type.96 = bf16[20,641,256]{1,2,0:T(8,128)(2,1)} reshape(bf16[20,641,128,2]{1,3,2,0:T(2,128)(2,1)} %copy.143) | data formatting | bytes 13127680 | tf_op jit(solution)/shard_map/convert_element_type | solution.py:138
  706.7 10.1 %copy.144 = bf16[20,641,256]{2,1,0:T(8,128)(2,1)} copy(bf16[20,641,256]{1,2,0:T(8,128)(2,1)} %convert_element_type.96) | data formatting | bytes 13127680 | tf_op jit(solution)/shard_map/convert_element_type | solution.py:138
  (78 shorter events, 84.1 us)
Async XLA Ops:
  0.0 320.4 %copy-start = (bf16[1,1024,1024]{2,1,0:T(8,128)(2,1)S(1)}, bf16[1,1024,1024]{2,1,0:T(8,128)(2,1)}, u32[]{:S(2)}) copy-start(bf16[1,1024,1024]{2,1,0:T(8,128)(2,1)} %param.12) | copy-start | bytes 6291460
  1.3 0.6 copy-start.7
  53.2 7.0 copy-start.10
  53.2 7.4 %copy-start.9 = (s32[3200,1]{0,1:T(1,128)S(1)}, s32[3200,1]{0,1:T(1,128)}, u32[]{:S(2)}) copy-start(s32[3200,1]{0,1:T(1,128)} %param.10) | copy-start | bytes 38404
  53.2 149.9 %all-to-all-start = ((bf16[40,128,2,320]{1,0,2,3:T(8,128)(2,1)}), bf16[40,128,2,320]{1,0,2,3:T(8,128)(2,1)}, u32[]{:S(2)}, u32[]{:S(2)}) async-start(bf16[40,128,2,320]{1,0,2,3:T(8,128)(2,1)} %copy.122), calls=%async_computation | async-start | bytes 13107200 | tf_op jit(solution)/shard_map/all_to_all | solution.py:107
  60.2 6.8 copy-start.12
  60.2 6.8 copy-start.11
  203.1 4.8 copy-start.5
  203.1 4.9 copy-start.6
  268.7 51.7 %all-to-all-start.1 = ((bf16[16,400,128]{2,1,0:T(8,128)(2,1)}), bf16[16,400,128]{2,1,0:T(8,128)(2,1)}, u32[]{:S(2)}, u32[]{:S(2)}) async-start(bf16[16,400,128]{2,1,0:T(8,128)(2,1)} %bitcast.128), calls=%async_computation.1 | async-start | bytes 3276800 | tf_op jit(solution)/shard_map/all_to_all | solution.py:123
  313.2 7.2 copy-start.13
  320.4 24.3 %copy-start.14 = (bf16[1,1024,128]{2,1,0:T(8,128)(2,1)S(1)}, bf16[1,1024,128]{2,1,0:T(8,128)(2,1)}, u32[]{:S(2)}) copy-start(bf16[1,1024,128]{2,1,0:T(8,128)(2,1)} %param.13) | copy-start | bytes 786436
  357.6 48.7 %all-to-all-start.2 = ((bf16[16,400,128]{2,1,0:T(8,128)(2,1)}), bf16[16,400,128]{2,1,0:T(8,128)(2,1)S(1)}, u32[]{:S(2)}, u32[]{:S(2)}) async-start(bf16[16,400,128]{2,1,0:T(8,128)(2,1)} %bitcast.129), calls=%async_computation.2 | async-start | bytes 3276800 | tf_op jit(solution)/shard_map/all_to_all | solution.py:127
  379.4 27.0 %copy-start.2 = (s32[3200]{0:T(1024)S(1)}, s32[3200]{0:T(1024)}, u32[]{:S(2)}) copy-start(s32[3200]{0:T(1024)} %get-tuple-element.5) | copy-start | bytes 38404
  441.2 14.2 %copy-start.3 = (bf16[640,1,1280]{2,0,1:T(8,128)(2,1)S(1)}, bf16[640,1,1280]{2,0,1:T(8,128)(2,1)}, u32[]{:S(2)}) copy-start(bf16[640,1,1280]{2,0,1:T(8,128)(2,1)} %get-tuple-element.18) | copy-start | bytes 4915204
  441.2 14.2 %copy-start.4 = (bf16[640,1,1280]{2,0,1:T(8,128)(2,1)S(1)}, bf16[640,1,1280]{2,0,1:T(8,128)(2,1)}, u32[]{:S(2)}) copy-start(bf16[640,1,1280]{2,0,1:T(8,128)(2,1)} %get-tuple-element.20) | copy-start | bytes 4915204
  653.1 1.1 copy-start.8
  706.7 10.1 %copy-start.1 = (bf16[1,1024,1024]{2,1,0:T(8,128)(2,1)S(1)}, bf16[1,1024,1024]{2,1,0:T(8,128)(2,1)}, u32[]{:S(2)}) copy-start(bf16[1,1024,1024]{2,1,0:T(8,128)(2,1)} %param.12) | copy-start | bytes 6291460
where the time goes:
time: 726 us; the launch traced here: 717 us
  local copies, waits for them, and re-layouts  270 us (37%)
  blocking collectives  149 us (21%)
  waiting for transfers between devices  119 us (16%)
  matrix products  84.6 us (12%)
  other arithmetic  75.7 us (10%)
  starting transfers between devices  18.3 us (3%)
    all_to_all x1, blocking collectives, on_device(): lax.all_to_all(fourier_out, 'wave', split_axis=0, concat_axis=3, tiled=True)  149 us
    all_to_all x1, waiting for transfers between devices, on_device(): lax.all_to_all(fourier_in, 'wave', split_axis=3, concat_axis=0, tiled=True)  119 us
    convert_element_type x3, local copies, waits for them, and re-layouts, on_device(): spectral_out = result.astype(jnp.bfloat16)  47 us
    slice x6, local copies, waits for them, and re-layouts, forcing(): jnp.roll(flattened, -1, axis=0)  46.4 us
    convert_element_type x1, local copies, waits for them, and re-layouts, on_device(): fourier_out = jnp.einsum('fal,qrl->qfra', tendency_grid, forward_table, p...  38.3 us
    reshape x2, local copies, waits for them, and re-layouts, on_device(): inverse_out.astype(jnp.bfloat16)  30.7 us
    concatenate x1, local copies, waits for them, and re-layouts, forcing(): jnp.roll(flattened, -1, axis=0)  26.9 us
    dot_general x1, matrix products, network(): jnp.dot(hidden, weight_mid, preferred_element_type=jnp.float32)  24.3 us
  transfers between devices with their start and end apart: 3, of which 1 were waited for; matrix products, arithmetic and copies ran while one was open for 16% of the time, Pallas kernels for 0%

commit v1 on v0

v1 whole, which is shorter than its diff:
```python
import functools
import math

import jax
import jax.numpy as jnp
from jax import lax
from jax.experimental import pallas as pl
from jax.experimental.pallas import tpu as pltpu
from jax.sharding import PartitionSpec as P

NLON = 1280
FIELDS = 4
SPREAD = ((0.375, 0.625, 0.0), (0.125, 0.875, 0.0), (0.0, 0.875, 0.125), (0.0, 0.625, 0.375))
VMEM_BYTES = 56 * 1024 * 1024


def params():
    return pltpu.CompilerParams(vmem_limit_bytes=VMEM_BYTES)


def slot_waves(pair_low, wave_total):
    return jnp.stack([pair_low, wave_total - 1 - pair_low], axis=1).reshape(-1)


def slot_positions(regimes, experts_total):
    onehot = (regimes[:, None] == jnp.arange(experts_total, dtype=jnp.int32)).astype(jnp.int32)
    ranking = jnp.cumsum(onehot, axis=0) - 1
    return jnp.sum(ranking * onehot, axis=1)


def zonal_tables(pair_low, wave_total, devices):
    waves = slot_waves(pair_low, wave_total).reshape(devices, 1, -1)
    quarter = jnp.array([0, NLON // 4], jnp.int32).reshape(1, 2, 1)
    rows = (devices, 2, waves.shape[2])
    waves_k = jnp.broadcast_to(waves, rows).reshape(-1)
    turn_k = jnp.broadcast_to(quarter, rows).reshape(-1)
    order = jnp.arange(NLON, dtype=jnp.int32)
    longitude = 4 * (order % (NLON // 4)) + order // (NLON // 4)

    def cosines(wave, turn, lon):
        phases = (wave * lon + turn) % NLON
        return jnp.cos(phases.astype(jnp.float32) * jnp.float32(2.0 * math.pi / NLON))

    scale = jnp.where(waves_k == 0, jnp.float32(1.0), jnp.float32(2.0))
    inverse = cosines(waves_k[None, :], turn_k[None, :], longitude[:, None]) * scale[None, :]
    forward = cosines(waves_k[:, None], turn_k[:, None], longitude[None, :]) * jnp.float32(
        1.0 / math.sqrt(NLON)
    )
    return inverse.astype(jnp.bfloat16), forward.astype(jnp.bfloat16)


def split_matrix(width):
    channel = jnp.arange(width, dtype=jnp.int32)
    target = (channel % 2) * (width // 2) + channel // 2
    return (target[:, None] == channel[None, :]).astype(jnp.bfloat16)


def group_of(count):
    return max(size for size in range(1, 6) if count % size == 0)


def inverse_legendre_kernel(pairs, lats, low, spec, leg, split, out, held):
    step = pl.program_id(0)
    group, degrees, channels = spec.shape
    feat = channels // 2
    lat_total = leg.shape[1]
    middle = (degrees - 1) // 2
    skip = middle // 256 * 256
    pair_steps = pairs // group

    @pl.when(step < pair_steps)
    def _():
        for g in range(group):
            pair = step * group + g
            lower = degrees - 1 - low[pair]
            coeffs = jnp.dot(spec[g], split[...], preferred_element_type=jnp.float32)
            tail = coeffs[middle:]
            on_first = lax.broadcasted_iota(jnp.int32, tail.shape, 0) < lower - middle
            first = jnp.concatenate([coeffs[:middle], jnp.where(on_first, tail, 0.0)], axis=0)
            second = jnp.concatenate(
                [jnp.zeros((middle - skip, channels), jnp.float32), jnp.where(on_first, 0.0, tail)],
                axis=0,
            )
            sides = (
                jnp.dot(leg[g], first.astype(jnp.bfloat16), preferred_element_type=jnp.float32),
                jnp.dot(
                    leg[g, :, skip:],
                    second.astype(jnp.bfloat16),
                    preferred_element_type=jnp.float32,
                ),
            )
            for s in range(2):
                for r in range(2):
                    start = (r * 2 * pairs + 2 * pair + s) * lat_total
                    held[pl.ds(pl.multiple_of(start, 8), lat_total), :] = sides[s][
                        :, r * feat : (r + 1) * feat
                    ]

    @pl.when(step >= pair_steps)
    def _():
        for d in range(out.shape[0]):
            first_lat = ((step - pair_steps) * out.shape[0] + d) * lats
            for a in range(lats):
                rows = held[pl.ds(first_lat + a, 4 * pairs, stride=lat_total), :]
                out[d, :, a * feat : (a + 1) * feat] = rows.astype(jnp.bfloat16)


def inverse_legendre(spectral, legendre, local_low, devices):
    pairs, degrees, channels = spectral.shape
    lat_total = legendre.shape[1]
    lats = lat_total // devices
    feat = channels // 2
    group, batch = group_of(pairs), group_of(devices)
    pair_steps = pairs // group
    last = pair_steps - 1
    return pl.pallas_call(
        functools.partial(inverse_legendre_kernel, pairs, lats),
        grid=(pair_steps + devices // batch,),
        in_specs=[
            pl.BlockSpec(memory_space=pltpu.SMEM),
            pl.BlockSpec((group, degrees, channels), lambda i: (jnp.minimum(i, last), 0, 0)),
            pl.BlockSpec((group, lat_total, degrees), lambda i: (jnp.minimum(i, last), 0, 0)),
            pl.BlockSpec((channels, channels), lambda i: (0, 0)),
        ],
        out_specs=pl.BlockSpec(
            (batch, 4 * pairs, lats * feat), lambda i: (jnp.maximum(i - pair_steps, 0), 0, 0)
        ),
        out_shape=jax.ShapeDtypeStruct((devices, 4 * pairs, lats * feat), jnp.bfloat16),
        scratch_shapes=[pltpu.VMEM((4 * pairs * lat_total, feat), jnp.float32)],
        compiler_params=params(),
        name="inverse_legendre",
    )(local_low, spectral, legendre, split_matrix(channels))


def to_grid_kernel(slots, table, coeffs, forced, packed, cols, sent):
    step = pl.program_id(0)
    quarter, feat = cols.shape[1:]

    @pl.when(step == 0)
    def _():
        sent[...] = jnp.zeros_like(sent)

    grid = jnp.dot(table[...], coeffs[...], preferred_element_type=jnp.float32)
    total = jnp.zeros((quarter, feat), jnp.float32)
    for t in range(2):
        field = grid[:, t * feat : (t + 1) * feat]
        forced[:, t * feat : (t + 1) * feat] = field * pltpu.roll(
            field, feat - feat // FIELDS, axis=1
        )
        for u in range(4):
            total = total + field[u * quarter : (u + 1) * quarter]
    before = jnp.maximum(step - 1, 0) * quarter
    held = cols.at[(step + 1) % 2]
    for k in range(quarter):
        sent[pl.ds(slots[before + k], 1), :] = held[pl.ds(k, 1), :]
    cols[step % 2] = (total * 0.125).astype(jnp.bfloat16).astype(jnp.float32)

    @pl.when(step == pl.num_programs(0) - 1)
    def _():
        for k in range(quarter):
            sent[pl.ds(slots[step * quarter + k], 1), :] = cols[step % 2, pl.ds(k, 1), :]
        packed[...] = sent[...].astype(jnp.bfloat16)


def to_grid(slots, table, coeffs, slot_total, feat):
    depth, lanes = coeffs.shape
    rows = lanes // (2 * feat)
    return pl.pallas_call(
        to_grid_kernel,
        grid_spec=pltpu.PrefetchScalarGridSpec(
            num_scalar_prefetch=1,
            grid=(rows,),
            in_specs=[
                pl.BlockSpec((NLON, depth), lambda i, s: (0, 0)),
                pl.BlockSpec((depth, 2 * feat), lambda i, s: (0, i)),
            ],
            out_specs=[
                pl.BlockSpec((NLON, 2 * feat), lambda i, s: (0, i)),
                pl.BlockSpec((slot_total, feat), lambda i, s: (0, 0)),
            ],
            scratch_shapes=[
                pltpu.VMEM((2, NLON // 4, feat), jnp.float32),
                pltpu.VMEM((slot_total, feat), jnp.float32),
            ],
        ),
        out_shape=[
            jax.ShapeDtypeStruct((NLON, lanes), jnp.float32),
            jax.ShapeDtypeStruct((slot_total, feat), jnp.bfloat16),
        ],
        compiler_params=params(),
        name="to_grid",
    )(slots, table, coeffs)


def silu(v):
    return 0.5 * v * (1.0 + jnp.tanh(0.5 * v))


def network_kernel(cols, weight_in, weight_mid, weight_out, out):
    rows = out.shape[0] // 2
    for half in range(2):
        own = slice(half * rows, (half + 1) * rows)
        hidden = jnp.dot(cols[own], weight_in[...], preferred_element_type=jnp.float32)
        hidden = silu(hidden).astype(jnp.bfloat16)
        deeper = jnp.dot(hidden, weight_mid[...], preferred_element_type=jnp.float32)
        deeper = silu(deeper).astype(jnp.bfloat16)
        result = jnp.dot(deeper, weight_out[...], preferred_element_type=jnp.float32)
        out[own] = result.astype(jnp.bfloat16)


def network(columns, weight_in, weight_mid, weight_out):
    rows, feat = columns.shape
    hid = weight_in.shape[1]
    block = rows // 8
    return pl.pallas_call(
        network_kernel,
        grid=(rows // block,),
        in_specs=[
            pl.BlockSpec((block, feat), lambda i: (i, 0)),
            pl.BlockSpec((feat, hid), lambda i: (0, 0)),
            pl.BlockSpec((hid, hid), lambda i: (0, 0)),
            pl.BlockSpec((hid, feat), lambda i: (0, 0)),
        ],
        out_specs=pl.BlockSpec((block, feat), lambda i: (i, 0)),
        out_shape=jax.ShapeDtypeStruct((rows, feat), jnp.bfloat16),
        compiler_params=params(),
        name="network",
    )(columns, weight_in, weight_mid, weight_out)


def to_waves_kernel(slots, table, forced, answers, out, wide, cols, tend):
    step = pl.program_id(0)
    quarter, feat = cols.shape[1:]

    @pl.when(step == 0)
    def _():
        wide[...] = answers[...].astype(jnp.float32)
        for k in range(quarter):
            cols[0, pl.ds(k, 1), :] = wide[pl.ds(slots[k], 1), :]

    coarse = cols[step % 2]
    after = jnp.minimum(step + 1, pl.num_programs(0) - 1) * quarter
    held = cols.at[(step + 1) % 2]
    for k in range(quarter):
        held[pl.ds(k, 1), :] = wide[pl.ds(slots[after + k], 1), :]
    before = pltpu.roll(coarse, 1, axis=0)
    following = pltpu.roll(coarse, quarter - 1, axis=0)
    for u in range(4):
        w, v, x = SPREAD[u]
        fine = v * coarse + (w * before if w else x * following)
        rows = slice(u * quarter, (u + 1) * quarter)
        for t in range(2):
            lanes = slice(t * feat, (t + 1) * feat)
            tend[rows, lanes] = (forced[rows, lanes] + fine).astype(jnp.bfloat16)
    out[...] = jnp.dot(table[...], tend[...], preferred_element_type=jnp.float32).astype(
        jnp.bfloat16
    )


def to_waves(slots, table, forced, answers):
    lanes = forced.shape[1]
    slot_total, feat = answers.shape
    depth = table.shape[0]
    rows = lanes // (2 * feat)
    return pl.pallas_call(
        to_waves_kernel,
        grid_spec=pltpu.PrefetchScalarGridSpec(
            num_scalar_prefetch=1,
            grid=(rows,),
            in_specs=[
                pl.BlockSpec((depth, NLON), lambda i, s: (0, 0)),
                pl.BlockSpec((NLON, 2 * feat), lambda i, s: (0, i)),
                pl.BlockSpec((slot_total, feat), lambda i, s: (0, 0)),
            ],
            out_specs=pl.BlockSpec((depth, 2 * feat), lambda i, s: (0, i)),
            scratch_shapes=[
                pltpu.VMEM((slot_total, feat), jnp.float32),
                pltpu.VMEM((2, NLON // 4, feat), jnp.float32),
                pltpu.VMEM((NLON, 2 * feat), jnp.bfloat16),
            ],
        ),
        out_shape=jax.ShapeDtypeStruct((depth, lanes), jnp.bfloat16),
        compiler_params=params(),
        name="to_waves",
    )(slots, table, forced, answers)


def forward_legendre_kernel(lats, low, coeffs, leg, merge, out, held):
    step = pl.program_id(0)
    group, degrees, channels = out.shape
    feat = channels // 2
    lat_total = leg.shape[2]
    batch, rows = coeffs.shape[:2]
    lat_steps = lat_total // (batch * lats)
    middle = (degrees - 1) // 2

    @pl.when(step < lat_steps)
    def _():
        for d in range(batch):
            first_lat = (step * batch + d) * lats
            for a in range(lats):
                held[pl.ds(first_lat + a, rows, stride=lat_total), :] = coeffs[
                    d, :, a * feat : (a + 1) * feat
                ].astype(jnp.float32)

    @pl.when(step >= lat_steps)
    def _():
        for g in range(group):
            pair = (step - lat_steps) * group + g
            lower = degrees - 1 - low[pair]
            sides = []
            for s in range(2):
                parts = []
                for r in range(2):
                    start = (r * (rows // 2) + 2 * pair + s) * lat_total
                    parts.append(held[pl.ds(pl.multiple_of(start, 8), lat_total), :])
                sides.append(jnp.concatenate(parts, axis=1).astype(jnp.bfloat16))
            first = jnp.dot(leg[g], sides[0], preferred_element_type=jnp.float32)
            second = jnp.dot(leg[g, middle:], sides[1], preferred_element_type=jnp.float32)
            on_first = lax.broadcasted_iota(jnp.int32, second.shape, 0) < lower - middle
            chosen = jnp.concatenate(
                [first[:middle], jnp.where(on_first, first[middle:], second)], axis=0
            )
            out[g] = jnp.dot(
                chosen.astype(jnp.bfloat16), merge[...], preferred_element_type=jnp.float32
            ).astype(jnp.bfloat16)


def forward_legendre(coeffs, legendre, local_low, channels):
    devices, rows, lanes = coeffs.shape
    pairs, degrees, lat_total = legendre.shape
    feat = channels // 2
    lats = lat_total // devices
    group, batch = group_of(pairs), group_of(devices)
    lat_steps = devices // batch
    return pl.pallas_call(
        functools.partial(forward_legendre_kernel, lats),
        grid=(lat_steps + pairs // group,),
        in_specs=[
            pl.BlockSpec(memory_space=pltpu.SMEM),
            pl.BlockSpec((batch, rows, lanes), lambda i: (jnp.minimum(i, lat_steps - 1), 0, 0)),
            pl.BlockSpec(
                (group, degrees, lat_total), lambda i: (jnp.maximum(i - lat_steps, 0), 0, 0)
            ),
            pl.BlockSpec((channels, channels), lambda i: (0, 0)),
        ],
        out_specs=pl.BlockSpec(
            (group, degrees, channels), lambda i: (jnp.maximum(i - lat_steps, 0), 0, 0)
        ),
        out_shape=jax.ShapeDtypeStruct((pairs, degrees, channels), jnp.bfloat16),
        scratch_shapes=[pltpu.VMEM((rows * lat_total, feat), jnp.float32)],
        compiler_params=params(),
        name="forward_legendre",
    )(local_low, coeffs, legendre, split_matrix(channels).T)


def exchange(blocks):
    return lax.all_to_all(blocks, "wave", split_axis=0, concat_axis=0, tiled=True)


def on_device(spectral, legendre, pair_low, routes, w_in, w_mid, w_out):
    pairs, degrees, channels = spectral.shape
    feat = channels // 2
    devices = lax.axis_size("wave")
    local_low = lax.dynamic_slice_in_dim(pair_low, lax.axis_index("wave") * pairs, pairs)

    sent = inverse_legendre(spectral, jnp.swapaxes(legendre, 1, 2), local_low, devices)
    arrived = exchange(sent)
    inverse_table, forward_table = zonal_tables(pair_low, degrees - 1, devices)
    regimes = routes[:, 0]
    capacity = 2 * regimes.shape[0] // devices
    slots = regimes * capacity + slot_positions(regimes, devices)

    forced, outgoing = to_grid(
        slots, inverse_table, arrived.reshape(-1, arrived.shape[2]), devices * capacity, feat
    )
    columns = exchange(outgoing.reshape(devices, capacity, feat))
    answers = network(columns.reshape(-1, feat), w_in[0], w_mid[0], w_out[0])
    incoming = exchange(answers.reshape(devices, capacity, feat)).reshape(-1, feat)
    waves = to_waves(slots, forward_table, forced, incoming)
    received = exchange(waves.reshape(arrived.shape))
    return forward_legendre(received, legendre, local_low, channels)


def solution(mesh):
    placed = (
        P(("grp", "wave"), None, None),
        P("wave", None, None),
        P(),
        P(("grp", "wave"), None),
        P("wave", None, None),
        P("wave", None, None),
        P("wave", None, None),
    )
    return jax.shard_map(
        on_device,
        mesh=mesh,
        in_specs=placed,
        out_specs=P(("grp", "wave"), None, None),
        check_vma=False,
    )
```

time: 726 us -> 500 us (0.69); the launches traced: 717 us -> 499 us
  local copies, waits for them, and re-layouts: 270 us -> 16.3 us
  Pallas kernels: 0 us -> 111 us
  waiting for transfers between devices: 119 us -> 213 us
  matrix products: 84.6 us -> 0 us
  blocking collectives: 149 us -> 86.7 us
  other arithmetic: 75.7 us -> 58.8 us
    pallas_call x0 -> x5, Pallas kernels: none -> 111 us  [the longest x1 25.5 us: network(): pl.pallas_call(network_kernel, grid=(rows // block,), in_specs=[pl.BlockS...]
    convert_element_type x5 -> x0, local copies, waits for them, and re-layouts: 95.1 us -> none  [the longest x3 47 us: on_device(): spectral_out = result.astype(jnp.bfloat16)]
    all_to_all x3 -> x2, waiting for transfers between devices: 119 us -> 213 us  [exchange(): lax.all_to_all(blocks, 'wave', split_axis=0, concat_axis=0, tiled=True)]
    dot_general x6 -> x0, matrix products: 84.6 us -> none  [the longest x1 24.3 us: network(): jnp.dot(hidden, weight_mid, preferred_element_type=jnp.float32)]
    all_to_all x1 -> x2, blocking collectives: 149 us -> 86.7 us  [exchange(): lax.all_to_all(blocks, 'wave', split_axis=0, concat_axis=0, tiled=True)]
    slice x6 -> x1, local copies, waits for them, and re-layouts: 46.4 us -> 0.46 us  [forcing(): jnp.roll(flattened, -1, axis=0)]
    reshape x3 -> x0, local copies, waits for them, and re-layouts: 38.8 us -> none  [the longest x2 30.7 us: on_device(): inverse_out.astype(jnp.bfloat16)]
    convert_element_type x3, other arithmetic: 15.8 us -> 53 us  [the longest x1 52.3 us: zonal_tables(): return (inverse.astype(jnp.bfloat16), forward.astype(jnp.bfloat16))]
  transfers between devices with their start and end apart: 3 -> 2, of which waited for: 1 -> 2; matrix products, arithmetic and copies ran while one was open for 16% -> 15% of each run, Pallas kernels for 0% -> 0%
where the time goes in v1:
time: 500 us; the launch traced here: 499 us
  waiting for transfers between devices  213 us (43%)
  Pallas kernels  111 us (22%)
  blocking collectives  86.7 us (17%)
  other arithmetic  58.8 us (12%)
  local copies, waits for them, and re-layouts  16.3 us (3%)
  starting transfers between devices  13.4 us (3%)
    all_to_all x2, waiting for transfers between devices, exchange(): lax.all_to_all(blocks, 'wave', split_axis=0, concat_axis=0, tiled=True)  213 us
    all_to_all x2, blocking collectives, exchange(): lax.all_to_all(blocks, 'wave', split_axis=0, concat_axis=0, tiled=True)  86.7 us
    convert_element_type x1, other arithmetic, zonal_tables(): return (inverse.astype(jnp.bfloat16), forward.astype(jnp.bfloat16))  52.3 us
    pallas_call x1, Pallas kernels, network(): pl.pallas_call(network_kernel, grid=(rows // block,), in_specs=[pl.BlockS...  25.5 us
    pallas_call x1, Pallas kernels, forward_legendre(): pl.pallas_call(functools.partial(forward_legendre_kernel, lats), grid=(la...  25.4 us
    pallas_call x1, Pallas kernels, inverse_legendre(): pl.pallas_call(functools.partial(inverse_legendre_kernel, pairs, lats), g...  21.7 us
    pallas_call x1, Pallas kernels, to_waves(): pl.pallas_call(to_waves_kernel, grid_spec=pltpu.PrefetchScalarGridSpec(nu...  19.1 us
    pallas_call x1, Pallas kernels, to_grid(): pl.pallas_call(to_grid_kernel, grid_spec=pltpu.PrefetchScalarGridSpec(num...  18.9 us
  transfers between devices with their start and end apart: 2, of which 2 were waited for; matrix products, arithmetic and copies ran while one was open for 15% of the time, Pallas kernels for 0%

profile of v1, /device:TPU:13, one launch (start us, length us, event | category | flops | bytes accessed | tf_op | source)
XLA Modules:
  0.0 498.9 jit_solution(11722398207401751745)
XLA Ops:
  0.0 0.7 fusion.18
  0.8 1.3 dynamic_slice.3.low
  2.1 21.7 %inverse_legendre.1 = bf16[16,80,2560]{2,1,0:T(8,128)(2,1)} custom-call(s32[20]{0:T(128)} %dynamic_slice.3.low, bf16[20,641,256]{2,1,0:T(8,128)(2,1)} %spec.1, bf16[20,320,641]{2,1,0:T(8,128)(2,1)} %bitcast.25, bf16[256,256]{1,0:T(8,128)(2,1)} %get-tuple-element.12.split), custom_call_target="tpu_custom_call" | custom-call | tf_op jit(solution)/shard_map/inverse_legendre/pallas_call | solution.py:116
  23.8 6.7 %all-to-all-start = ((bf16[16,80,2560]{2,1,0:T(8,128)(2,1)}), bf16[16,80,2560]{2,1,0:T(8,128)(2,1)}, u32[]{:S(2)}, u32[]{:S(2)}) async-start(bf16[16,80,2560]{2,1,0:T(8,128)(2,1)} %inverse_legendre.1), calls=%async_computation | async-start | bytes 13107200 | tf_op jit(solution)/shard_map/all_to_all | solution.py:358
  30.8 0.1 copy.10
  30.9 0.1 broadcast_in_dim.14
  31.1 0.1 mul.90
  31.2 4.6 reduce-window.6
  35.8 0.5 slice_reduce_fusion
  36.3 0.2 reduce-window.9
  36.5 0.1 add_add_fusion
  36.6 0.1 fusion.20
  36.8 0.6 multiply_add_fusion.slots
  37.4 52.3 %fusion.9 = (bf16[1280,1280]{1,0:T(8,128)(2,1)}, bf16[1280,1280]{1,0:T(8,128)(2,1)}) fusion(f32[1280]{0:T(1024)S(1)} %compare_select_fusion, s32[1280]{0:T(1024)S(1)} %add.108, s32[1280]{0:T(1024)S(1)} %fusion.27, s32[1280]{0:T(1024)S(1)} %mul.90), kind=kLoop, calls=%fused_computation.11 | loop fusion | flops 39321600 | bytes 6574080 | tf_op jit(solution)/shard_map/convert_element_type | solution.py:49
  89.6 83.9 %all-to-all-done = bf16[16,80,2560]{2,1,0:T(8,128)(2,1)} async-done(((bf16[16,80,2560]{2,1,0:T(8,128)(2,1)}), bf16[16,80,2560]{2,1,0:T(8,128)(2,1)}, u32[]{:S(2)}, u32[]{:S(2)}) %all-to-all-start) | async-done | bytes 6553632 | tf_op jit(solution)/shard_map/all_to_all | solution.py:358
  173.5 18.9 %to_grid.1 = (f32[1280,2560]{1,0:T(8,128)}, bf16[6400,128]{1,0:T(8,128)(2,1)}) custom-call(s32[3200]{0:T(1024)} %multiply_add_fusion.slots, bf16[1280,1280]{1,0:T(8,128)(2,1)} %get-tuple-element.9.table, bf16[1280,2560]{1,0:T(8,128)(2,1)} %bitcast.2.coeffs), custom_call_target="tpu_custom_call" | custom-call | tf_op jit(solution)/shard_map/to_grid/pallas_call | solution.py:168
  192.4 42.6 %all_to_all.20 = bf16[16,400,128]{2,1,0:T(8,128)(2,1)} all-to-all(bf16[16,400,128]{2,1,0:T(8,128)(2,1)} %bitcast.31), channel_id=1, replica_groups=mesh['grp'=2,'wave'=16] {'wave'}, dimensions={0} | all-to-all | bytes 3276800 | tf_op jit(solution)/shard_map/all_to_all | solution.py:358
  235.0 25.5 %network.1 = bf16[6400,128]{1,0:T(8,128)(2,1)} custom-call(bf16[6400,128]{1,0:T(8,128)(2,1)} %bitcast.27, bf16[128,1024]{1,0:T(8,128)(2,1)} %bitcast.33, bf16[1024,1024]{1,0:T(8,128)(2,1)} %bitcast.30, bf16[1024,128]{1,0:T(8,128)(2,1)} %bitcast.34), custom_call_target="tpu_custom_call" | custom-call | tf_op jit(solution)/shard_map/network/pallas_call | solution.py:215
  260.5 44.1 %all_to_all.21 = bf16[16,400,128]{2,1,0:T(8,128)(2,1)} all-to-all(bf16[16,400,128]{2,1,0:T(8,128)(2,1)} %bitcast.28), channel_id=1, replica_groups=mesh['grp'=2,'wave'=16] {'wave'}, dimensions={0} | all-to-all | bytes 3276800 | tf_op jit(solution)/shard_map/all_to_all | solution.py:358
  304.6 19.1 %to_waves.1 = bf16[1280,2560]{1,0:T(8,128)(2,1)} custom-call(s32[3200]{0:T(1024)} %multiply_add_fusion.slots, bf16[1280,1280]{1,0:T(8,128)(2,1)} %get-tuple-element.10.table, f32[1280,2560]{1,0:T(8,128)} %get-tuple-element.7.forced, bf16[6400,128]{1,0:T(8,128)(2,1)} %bitcast.29), custom_call_target="tpu_custom_call" | custom-call | tf_op jit(solution)/shard_map/to_waves/pallas_call | solution.py:265
  323.7 6.7 %all-to-all-start.3 = ((bf16[16,80,2560]{2,1,0:T(8,128)(2,1)}), bf16[16,80,2560]{2,1,0:T(8,128)(2,1)}, u32[]{:S(2)}, u32[]{:S(2)}) async-start(bf16[16,80,2560]{2,1,0:T(8,128)(2,1)} %bitcast.26), calls=%async_computation.3 | async-start | bytes 13107200 | tf_op jit(solution)/shard_map/all_to_all | solution.py:358
  330.4 14.0 %copy.11.leg = bf16[20,641,320]{2,1,0:T(8,128)(2,1)} copy(bf16[20,641,320]{1,2,0:T(8,128)(2,1)} %param.9) | data formatting | bytes 16409600 | tf_op args[1]
  344.4 129.0 %all-to-all-done.3.coeffs = bf16[16,80,2560]{2,1,0:T(8,128)(2,1)} async-done(((bf16[16,80,2560]{2,1,0:T(8,128)(2,1)}), bf16[16,80,2560]{2,1,0:T(8,128)(2,1)}, u32[]{:S(2)}, u32[]{:S(2)}) %all-to-all-start.3) | async-done | bytes 6553632 | tf_op jit(solution)/shard_map/all_to_all | solution.py:358
  473.4 25.4 %forward_legendre.1 = bf16[20,641,256]{2,1,0:T(8,128)(2,1)} custom-call(s32[20]{0:T(128)} %dynamic_slice.3.low, bf16[16,80,2560]{2,1,0:T(8,128)(2,1)} %all-to-all-done.3.coeffs, bf16[20,641,320]{2,1,0:T(8,128)(2,1)} %copy.11.leg, bf16[256,256]{1,0:T(8,128)(2,1)} %get-tuple-element.11.merge), custom_call_target="tpu_custom_call" | custom-call | tf_op jit(solution)/shard_map/forward_legendre/pallas_call | solution.py:336
  (17 shorter events, 0.3 us)
Async XLA Ops:
  23.8 6.7 %copy-start.1 = (s32[320]{0:T(512)S(1)}, s32[320]{0:T(512)}, u32[]{:S(2)}) copy-start(s32[320]{0:T(512)} %param.10) | copy-start | bytes 3844
  23.8 6.9 %copy-start = (s32[3200,1]{0,1:T(1,128)S(1)}, s32[3200,1]{0,1:T(1,128)}, u32[]{:S(2)}) copy-start(s32[3200,1]{0,1:T(1,128)} %param.11) | copy-start | bytes 38404
  23.8 149.7 %all-to-all-start = ((bf16[16,80,2560]{2,1,0:T(8,128)(2,1)}), bf16[16,80,2560]{2,1,0:T(8,128)(2,1)}, u32[]{:S(2)}, u32[]{:S(2)}) async-start(bf16[16,80,2560]{2,1,0:T(8,128)(2,1)} %inverse_legendre.1), calls=%async_computation | async-start | bytes 13107200 | tf_op jit(solution)/shard_map/all_to_all | solution.py:358
  323.7 149.7 %all-to-all-start.3 = ((bf16[16,80,2560]{2,1,0:T(8,128)(2,1)}), bf16[16,80,2560]{2,1,0:T(8,128)(2,1)}, u32[]{:S(2)}, u32[]{:S(2)}) async-start(bf16[16,80,2560]{2,1,0:T(8,128)(2,1)} %bitcast.26), calls=%async_computation.3 | async-start | bytes 13107200 | tf_op jit(solution)/shard_map/all_to_all | solution.py:358

commit v2 on v1

v2 whole, which is shorter than its diff:
```python
import functools
import math

import jax
import jax.numpy as jnp
from jax import lax
from jax.experimental import pallas as pl
from jax.experimental.pallas import tpu as pltpu
from jax.sharding import PartitionSpec as P

NLON = 1280
FIELDS = 4
SPREAD = ((0.375, 0.625, 0.0), (0.125, 0.875, 0.0), (0.0, 0.875, 0.125), (0.0, 0.625, 0.375))
PITCH_EXTRA = 8


def params(mebibytes):
    return pltpu.CompilerParams(vmem_limit_bytes=mebibytes * 1024 * 1024)


def slot_positions(regimes, experts_total):
    onehot = (regimes[:, None] == jnp.arange(experts_total, dtype=jnp.int32)).astype(jnp.int32)
    ranking = jnp.cumsum(onehot, axis=0) - 1
    return jnp.sum(ranking * onehot, axis=1)


def zonal_tables(pair_low, wave_total):
    other = wave_total - 1 - pair_low
    even = jnp.where(pair_low % 2 == 0, pair_low, other)
    waves = jnp.stack([even, wave_total - 1 - even]).reshape(2, -1, 1)
    quarter = jnp.array([0, NLON // 4], jnp.int32).reshape(1, 1, 2)
    rows = (2, waves.shape[1], 2)
    waves_k = jnp.broadcast_to(waves, rows).reshape(2, -1)
    turn_k = jnp.broadcast_to(quarter, rows).reshape(2, -1)
    order = jnp.arange(NLON // 2, dtype=jnp.int32)
    longitude = 4 * (order % (NLON // 8)) + order // (NLON // 8)

    def cosines(wave, turn, lon):
        phases = (wave * lon + turn) % NLON
        return jnp.cos(phases.astype(jnp.float32) * jnp.float32(2.0 * math.pi / NLON))

    scale = jnp.where(waves_k == 0, jnp.float32(1.0), jnp.float32(2.0))
    inverse = scale[:, None, :] * cosines(
        waves_k[:, None, :], turn_k[:, None, :], longitude[None, :, None]
    )
    forward = jnp.float32(1.0 / math.sqrt(NLON)) * cosines(
        waves_k[:, :, None], turn_k[:, :, None], longitude[None, None, :]
    )
    return inverse.astype(jnp.bfloat16), forward.astype(jnp.bfloat16)


def lats_together(lats):
    return 4 if lats % 4 == 0 else 2


def lane_start(lat, parity, lats, feat):
    together = lats_together(lats)
    return ((lat // together * 2 + parity) * together + lat % together) * feat


def in_vmem(array):
    return pltpu.with_memory_space_constraint(array, pltpu.VMEM)


WHOLE = pl.BlockSpec(memory_space=pltpu.VMEM)


def split_matrix(width):
    channel = jnp.arange(width, dtype=jnp.int32)
    target = (channel % 2) * (width // 2) + channel // 2
    return (target[:, None] == channel[None, :]).astype(jnp.bfloat16)


def group_of(pairs):
    return 4 if pairs % 4 == 0 else pairs


def staggered(step, steps, first, second, slots):
    @pl.when(step == 0)
    def _():
        first(0, slots[0])

    for odd in range(2):

        @pl.when((step > 0) & (step < steps) & (step % 2 == odd))
        def _(odd=odd):
            second(step - 1, slots[1 - odd])
            first(step, slots[odd])

    @pl.when(step == steps)
    def _():
        second(steps - 1, slots[(steps - 1) % 2])


def inverse_legendre_kernel(steps, low, spec, leg, split, out, *slots):
    step = pl.program_id(0)
    group, degrees, channels = spec.shape
    feat = channels // 2
    lat_total = leg.shape[1]
    devices, rows = out.shape[:2]
    lats = lat_total // devices
    pitch = lat_total + PITCH_EXTRA
    middle = (degrees - 1) // 2
    skip = middle // 256 * 256

    def transform(number, held):
        for g in range(group):
            own_low = low[number * group + g]
            lower = degrees - 1 - own_low
            coeffs = jnp.dot(spec[g], split[...], preferred_element_type=jnp.float32)
            tail = coeffs[middle:]
            on_first = lax.broadcasted_iota(jnp.int32, tail.shape, 0) < lower - middle
            first = jnp.concatenate([coeffs[:middle], jnp.where(on_first, tail, 0.0)], axis=0)
            second = jnp.concatenate(
                [jnp.zeros((middle - skip, channels), jnp.float32), jnp.where(on_first, 0.0, tail)],
                axis=0,
            )
            sides = (
                jnp.dot(leg[g], first.astype(jnp.bfloat16), preferred_element_type=jnp.float32),
                jnp.dot(
                    leg[g, :, skip:],
                    second.astype(jnp.bfloat16),
                    preferred_element_type=jnp.float32,
                ),
            )
            for s in range(2):
                parity = (own_low + s) % 2
                for r in range(2):
                    start = (parity * rows + 2 * g + r) * pitch
                    held[pl.ds(pl.multiple_of(start, 8), lat_total), :] = sides[s][
                        :, r * feat : (r + 1) * feat
                    ]

    def turn(_, held):
        for d in range(devices):
            for a in range(lats):
                for parity in range(2):
                    start = parity * rows * pitch + d * lats + a
                    own = held[pl.ds(start, rows, stride=pitch), :]
                    lane = lane_start(a, parity, lats, feat)
                    out[d, :, lane : lane + feat] = own.astype(jnp.bfloat16)

    staggered(step, steps, transform, turn, slots)


def inverse_legendre(spectral, legendre, local_low, devices):
    pairs, degrees, channels = spectral.shape
    lat_total = legendre.shape[1]
    lanes = lat_total // devices * channels
    group = group_of(pairs)
    steps = pairs // group
    slot = pltpu.VMEM((4 * group * (lat_total + PITCH_EXTRA), channels // 2), jnp.float32)
    return pl.pallas_call(
        functools.partial(inverse_legendre_kernel, steps),
        grid=(steps + 1,),
        in_specs=[
            pl.BlockSpec(memory_space=pltpu.SMEM),
            pl.BlockSpec((group, degrees, channels), lambda i: (jnp.minimum(i, steps - 1), 0, 0)),
            pl.BlockSpec((group, lat_total, degrees), lambda i: (jnp.minimum(i, steps - 1), 0, 0)),
            pl.BlockSpec((channels, channels), lambda i: (0, 0)),
        ],
        out_specs=pl.BlockSpec(
            (devices, 2 * group, lanes), lambda i: (0, jnp.maximum(i - 1, 0), 0)
        ),
        out_shape=jax.ShapeDtypeStruct((devices, 2 * pairs, lanes), jnp.bfloat16),
        scratch_shapes=[slot, slot],
        compiler_params=params(40),
        name="inverse_legendre",
    )(local_low, spectral, legendre, split_matrix(channels))


def to_grid_kernel(steps, slots, table, coeffs, forced, packed, cols, sent, *held):
    step = pl.program_id(0)
    count, feat = cols.shape
    lanes = forced.shape[2]
    half = table.shape[1]
    eighth = half // 4
    lat_rows = lanes // (2 * feat)

    def transform(number, parts):
        for parity in range(2):
            start = pl.multiple_of((2 * number + parity) * lanes, lanes)
            parts[parity] = jnp.dot(
                table[parity],
                coeffs[:, pl.ds(start, lanes)],
                preferred_element_type=jnp.float32,
            )

    def finish(number, parts):
        for i in range(lat_rows):
            totals = [jnp.zeros((eighth, feat), jnp.float32) for _ in range(2)]
            for t in (2 * i, 2 * i + 1):
                own = slice(t * feat, (t + 1) * feat)
                for u in range(4):
                    rows = slice(u * eighth, (u + 1) * eighth)
                    even, odd = parts[0, rows, own], parts[1, rows, own]
                    for h, field in enumerate((even + odd, even - odd)):
                        totals[h] = totals[h] + field
                        start = h * half + u * eighth
                        forced[number, start : start + eighth, own] = field * pltpu.roll(
                            field, feat - feat // FIELDS, axis=1
                        )
            for h in range(2):
                start = (2 * i + h) * eighth
                cols[start : start + eighth, :] = (
                    (totals[h] * 0.125).astype(jnp.bfloat16).astype(jnp.float32)
                )
        for k in range(count):
            sent[pl.ds(slots[number * count + k], 1), :] = cols[pl.ds(k, 1), :]

    @pl.when(step == 0)
    def _():
        sent[...] = jnp.zeros_like(sent)

    staggered(step, steps, transform, finish, held)

    @pl.when(step == steps)
    def _():
        packed[...] = sent[...].astype(jnp.bfloat16)


def to_grid(slots, table, coeffs, slot_total, feat):
    depth, lanes = coeffs.shape
    lats = lanes // (2 * feat)
    together = lats_together(lats)
    own = together * feat
    count = together // 2 * (NLON // 4)
    steps = lats // together
    part = pltpu.VMEM((2, NLON // 2, own), jnp.float32)
    return pl.pallas_call(
        functools.partial(to_grid_kernel, steps),
        grid_spec=pltpu.PrefetchScalarGridSpec(
            num_scalar_prefetch=1,
            grid=(steps + 1,),
            in_specs=[
                pl.BlockSpec((2, NLON // 2, depth), lambda i, s: (0, 0, 0)),
                WHOLE,
            ],
            out_specs=[WHOLE, pl.BlockSpec((slot_total, feat), lambda i, s: (0, 0))],
            scratch_shapes=[
                pltpu.VMEM((count, feat), jnp.float32),
                pltpu.VMEM((slot_total, feat), jnp.float32),
                part,
                part,
            ],
        ),
        out_shape=[
            pltpu.VMEM((steps, NLON, own), jnp.float32),
            jax.ShapeDtypeStruct((slot_total, feat), jnp.bfloat16),
        ],
        compiler_params=params(30),
        name="to_grid",
    )(slots, table, in_vmem(coeffs))


def silu(v):
    return 0.5 * v * (1.0 + jnp.tanh(0.5 * v))


def network_kernel(cols, weight_in, weight_mid, weight_out, out):
    rows = out.shape[0] // 2
    for half in range(2):
        own = slice(half * rows, (half + 1) * rows)
        hidden = jnp.dot(cols[own], weight_in[...], preferred_element_type=jnp.float32)
        hidden = silu(hidden).astype(jnp.bfloat16)
        deeper = jnp.dot(hidden, weight_mid[...], preferred_element_type=jnp.float32)
        deeper = silu(deeper).astype(jnp.bfloat16)
        result = jnp.dot(deeper, weight_out[...], preferred_element_type=jnp.float32)
        out[own] = result.astype(jnp.bfloat16)


def network(columns, weight_in, weight_mid, weight_out):
    rows, feat = columns.shape
    hid = weight_in.shape[1]
    block = rows // 8
    return pl.pallas_call(
        network_kernel,
        grid=(rows // block,),
        in_specs=[
            pl.BlockSpec((block, feat), lambda i: (i, 0)),
            pl.BlockSpec((feat, hid), lambda i: (0, 0)),
            pl.BlockSpec((hid, hid), lambda i: (0, 0)),
            pl.BlockSpec((hid, feat), lambda i: (0, 0)),
        ],
        out_specs=pl.BlockSpec((block, feat), lambda i: (i, 0)),
        out_shape=jax.ShapeDtypeStruct((rows, feat), jnp.bfloat16),
        compiler_params=params(30),
        name="network",
    )(columns, weight_in, weight_mid, weight_out)


def to_waves_kernel(steps, slots, table, forced, answers, out, wide, *held):
    step = pl.program_id(0)
    count, feat = held[1].shape
    lanes = forced.shape[2]
    half = table.shape[2]
    eighth = half // 4
    quarter = 2 * eighth

    def collect(number, cols):
        for k in range(count):
            cols[pl.ds(k, 1), :] = wide[pl.ds(slots[number * count + k], 1), :]

    def fold(number, slot):
        folded, cols, next_cols = slot
        for i in range(count // quarter):
            coarse = cols[i * quarter : (i + 1) * quarter, :]
            before = pltpu.roll(coarse, 1, axis=0)
            following = pltpu.roll(coarse, quarter - 1, axis=0)
            for u in range(4):
                w, v, x = SPREAD[u]
                fine = v * coarse + (w * before if w else x * following)
                rows = slice(u * eighth, (u + 1) * eighth)
                far_rows = slice(half + u * eighth, half + (u + 1) * eighth)
                for t in (2 * i, 2 * i + 1):
                    own = slice(t * feat, (t + 1) * feat)
                    near = forced[number, rows, own] + fine[:eighth]
                    far = forced[number, far_rows, own] + fine[eighth:]
                    folded[0, rows, own] = (near + far).astype(jnp.bfloat16)
                    folded[1, rows, own] = (near - far).astype(jnp.bfloat16)
        collect(jnp.minimum(number + 1, steps - 1), next_cols)

    def transform(_, slot):
        folded = slot[0]
        for parity in range(2):
            out[:, parity * lanes : (parity + 1) * lanes] = jnp.dot(
                table[parity], folded[parity], preferred_element_type=jnp.float32
            ).astype(jnp.bfloat16)

    @pl.when(step == 0)
    def _():
        wide[...] = answers[...].astype(jnp.float32)
        collect(0, held[1])

    staggered(
        step,
        steps,
        fold,
        transform,
        ((held[0], held[1], held[3]), (held[2], held[3], held[1])),
    )


def to_waves(slots, table, forced, answers):
    steps, _, own = forced.shape
    slot_total, feat = answers.shape
    depth = table.shape[1]
    count = own // feat // 2 * (NLON // 4)
    slot = [
        pltpu.VMEM((2, NLON // 2, own), jnp.bfloat16),
        pltpu.VMEM((count, feat), jnp.float32),
    ]
    return pl.pallas_call(
        functools.partial(to_waves_kernel, steps),
        grid_spec=pltpu.PrefetchScalarGridSpec(
            num_scalar_prefetch=1,
            grid=(steps + 1,),
            in_specs=[
                pl.BlockSpec((2, depth, NLON // 2), lambda i, s: (0, 0, 0)),
                WHOLE,
                pl.BlockSpec((slot_total, feat), lambda i, s: (0, 0)),
            ],
            out_specs=pl.BlockSpec((depth, 2 * own), lambda i, s: (0, jnp.maximum(i - 1, 0))),
            scratch_shapes=[
                pltpu.VMEM((slot_total, feat), jnp.float32),
                *slot,
                *slot,
            ],
        ),
        out_shape=jax.ShapeDtypeStruct((depth, 2 * steps * own), jnp.bfloat16),
        compiler_params=params(30),
        name="to_waves",
    )(slots, table, in_vmem(forced), answers)


def forward_legendre_kernel(steps, low, coeffs, leg, merge, out, *slots):
    step = pl.program_id(0)
    group, degrees, channels = out.shape
    feat = channels // 2
    lat_total = leg.shape[2]
    devices, rows = coeffs.shape[0], 2 * group
    lats = lat_total // devices
    pitch = lat_total + PITCH_EXTRA
    middle = (degrees - 1) // 2

    def turn(number, held):
        own_rows = slice(None)
        if coeffs.shape[1] > rows:
            own_rows = pl.ds(pl.multiple_of(number * rows, rows), rows)
        for d in range(devices):
            for a in range(lats):
                for parity in range(2):
                    start = parity * rows * pitch + d * lats + a
                    lane = lane_start(a, parity, lats, feat)
                    held[pl.ds(start, rows, stride=pitch), :] = coeffs[
                        d, own_rows, lane : lane + feat
                    ].astype(jnp.float32)

    def transform(number, held):
        for g in range(group):
            own_low = low[number * group + g]
            lower = degrees - 1 - own_low
            sides = []
            for s in range(2):
                parity = (own_low + s) % 2
                parts = []
                for r in range(2):
                    start = (parity * rows + 2 * g + r) * pitch
                    parts.append(held[pl.ds(pl.multiple_of(start, 8), lat_total), :])
                sides.append(jnp.concatenate(parts, axis=1).astype(jnp.bfloat16))
            first = jnp.dot(leg[number * group + g], sides[0], preferred_element_type=jnp.float32)
            second = jnp.dot(leg[number * group + g, middle:], sides[1], preferred_element_type=jnp.float32)
            on_first = lax.broadcasted_iota(jnp.int32, second.shape, 0) < lower - middle
            chosen = jnp.concatenate(
                [first[:middle], jnp.where(on_first, first[middle:], second)], axis=0
            )
            out[g] = jnp.dot(
                chosen.astype(jnp.bfloat16), merge[...], preferred_element_type=jnp.float32
            ).astype(jnp.bfloat16)

    staggered(step, steps, turn, transform, slots)


def forward_legendre(coeffs, legendre, local_low, channels):
    devices, rows, lanes = coeffs.shape
    pairs, degrees, lat_total = legendre.shape
    group = group_of(pairs)
    steps = pairs // group
    slot = pltpu.VMEM((4 * group * (lat_total + PITCH_EXTRA), channels // 2), jnp.float32)
    return pl.pallas_call(
        functools.partial(forward_legendre_kernel, steps),
        grid=(steps + 1,),
        in_specs=[
            pl.BlockSpec(memory_space=pltpu.SMEM),
            WHOLE,
            WHOLE,
            pl.BlockSpec((channels, channels), lambda i: (0, 0)),
        ],
        out_specs=pl.BlockSpec((group, degrees, channels), lambda i: (jnp.maximum(i - 1, 0), 0, 0)),
        out_shape=jax.ShapeDtypeStruct((pairs, degrees, channels), jnp.bfloat16),
        scratch_shapes=[slot, slot],
        compiler_params=params(30),
        name="forward_legendre",
    )(local_low, in_vmem(coeffs), in_vmem(legendre), split_matrix(channels).T)


def exchange(blocks):
    return lax.all_to_all(blocks, "wave", split_axis=0, concat_axis=0, tiled=True)


def on_device(spectral, legendre, pair_low, routes, w_in, w_mid, w_out):
    pairs, degrees, channels = spectral.shape
    feat = channels // 2
    devices = lax.axis_size("wave")
    local_low = lax.dynamic_slice_in_dim(pair_low, lax.axis_index("wave") * pairs, pairs)

    sent = inverse_legendre(spectral, jnp.swapaxes(legendre, 1, 2), local_low, devices)
    arrived = exchange(sent)
    inverse_table, forward_table = zonal_tables(pair_low, degrees - 1)
    regimes = routes[:, 0]
    capacity = 2 * regimes.shape[0] // devices
    slots = regimes * capacity + slot_positions(regimes, devices)

    forced, outgoing = to_grid(
        slots, inverse_table, arrived.reshape(-1, arrived.shape[2]), devices * capacity, feat
    )
    columns = exchange(outgoing.reshape(devices, capacity, feat))
    answers = network(columns.reshape(-1, feat), w_in[0], w_mid[0], w_out[0])
    incoming = exchange(answers.reshape(devices, capacity, feat)).reshape(-1, feat)
    waves = to_waves(slots, forward_table, forced, incoming)
    received = exchange(waves.reshape(arrived.shape))
    return forward_legendre(received, legendre, local_low, channels)


def solution(mesh):
    placed = (
        P(("grp", "wave"), None, None),
        P("wave", None, None),
        P(),
        P(("grp", "wave"), None),
        P("wave", None, None),
        P("wave", None, None),
        P("wave", None, None),
    )
    return jax.shard_map(
        on_device,
        mesh=mesh,
        in_specs=placed,
        out_specs=P(("grp", "wave"), None, None),
        check_vma=False,
    )
```

time: 500 us -> 487 us (0.974)
  Pallas kernels: 111 us -> 79 us
  other arithmetic: 58.8 us -> 31.2 us
  waiting for transfers between devices: 213 us -> 240 us
  local copies, waits for them, and re-layouts: 16.3 us -> 37.4 us
    pallas_call x4, Pallas kernels: 85.1 us -> 55.7 us  [the longest x1 14.7 us: forward_legendre(): pl.pallas_call(functools.partial(forward_legendre_kernel, steps), grid=(s...]
    all_to_all x2, waiting for transfers between devices: 213 us -> 240 us  [exchange(): lax.all_to_all(blocks, 'wave', split_axis=0, concat_axis=0, tiled=True)]
    convert_element_type x1, other arithmetic: 52.3 us -> 25.9 us  [zonal_tables(): return (inverse.astype(jnp.bfloat16), forward.astype(jnp.bfloat16))]
    unnamed x5 -> x23, local copies, waits for them, and re-layouts: 14 us -> 35.6 us
  transfers between devices with their start and end apart: 2 -> 2, of which waited for: 2 -> 2; matrix products, arithmetic and copies ran while one was open for 15% -> 9% of each run, Pallas kernels for 0% -> 0%
where the time goes in v2:
time: 487 us; the launch traced here: 486 us
  waiting for transfers between devices  240 us (49%)
  blocking collectives  85.2 us (17%)
  Pallas kernels  79 us (16%)
  local copies, waits for them, and re-layouts  37.4 us (8%)
  other arithmetic  31.2 us (6%)
  starting transfers between devices  13.4 us (3%)
    all_to_all x2, waiting for transfers between devices, exchange(): lax.all_to_all(blocks, 'wave', split_axis=0, concat_axis=0, tiled=True)  240 us
    all_to_all x2, blocking collectives, exchange(): lax.all_to_all(blocks, 'wave', split_axis=0, concat_axis=0, tiled=True)  85.2 us
    unnamed x23, local copies, waits for them, and re-layouts  35.6 us
    convert_element_type x1, other arithmetic, zonal_tables(): return (inverse.astype(jnp.bfloat16), forward.astype(jnp.bfloat16))  25.9 us
    pallas_call x1, Pallas kernels, network(): pl.pallas_call(network_kernel, grid=(rows // block,), in_specs=[pl.BlockS...  23.2 us
    pallas_call x1, Pallas kernels, forward_legendre(): pl.pallas_call(functools.partial(forward_legendre_kernel, steps), grid=(s...  14.7 us
    pallas_call x1, Pallas kernels, inverse_legendre(): pl.pallas_call(functools.partial(inverse_legendre_kernel, steps), grid=(s...  14.4 us
    pallas_call x1, Pallas kernels, to_waves(): pl.pallas_call(functools.partial(to_waves_kernel, steps), grid_spec=pltpu...  13.6 us
  transfers between devices with their start and end apart: 2, of which 2 were waited for; matrix products, arithmetic and copies ran while one was open for 9% of the time, Pallas kernels for 0%

profile of v2, /device:TPU:13, one launch (start us, length us, event | category | flops | bytes accessed | tf_op | source)
XLA Modules:
  0.0 486.2 jit_solution(15218359339582564059)
XLA Ops:
  0.1 0.8 dynamic_slice.3.low
  0.9 2.9 copy-done.5
  3.8 14.4 %inverse_legendre.1 = bf16[16,40,5120]{2,1,0:T(8,128)(2,1)S(1)} custom-call(s32[20]{0:T(128)S(1)} %dynamic_slice.3.low, bf16[20,641,256]{2,1,0:T(8,128)(2,1)S(1)} %copy-done.5, bf16[20,320,641]{2,1,0:T(8,128)(2,1)} %bitcast.33, bf16[256,256]{1,0:T(8,128)(2,1)S(1)} %get-tuple-element.14.split), custom_call_target="tpu_custom_call" | custom-call | tf_op jit(solution)/shard_map/inverse_legendre/pallas_call | solution.py:153
  18.2 2.8 copy-done.1
  21.0 6.7 %all-to-all-start = ((bf16[16,40,5120]{2,1,0:T(8,128)(2,1)}), bf16[16,40,5120]{2,1,0:T(8,128)(2,1)}, u32[]{:S(2)}, u32[]{:S(2)}) async-start(bf16[16,40,5120]{2,1,0:T(8,128)(2,1)} %copy-done.1), calls=%async_computation | async-start | bytes 13107200 | tf_op jit(solution)/shard_map/all_to_all | solution.py:448
  27.9 4.6 reduce-window.6
  32.6 0.5 slice_reduce_fusion
  33.0 0.2 reduce-window.9
  33.4 0.2 mul.90
  33.9 25.9 %fusion.9 = (bf16[2,640,640]{2,1,0:T(8,128)(2,1)S(1)}, bf16[2,640,640]{2,1,0:T(8,128)(2,1)S(1)}) fusion(s32[640]{0:T(1024)S(1)} %broadcast_in_dim.16, s32[640]{0:T(1024)S(1)} %fusion.27, s32[2,640]{1,0:T(2,128)S(1)} %mul.90, f32[2,640]{1,0:T(2,128)S(1)} %compare_select_fusion), kind=kLoop, calls=%fused_computation.11 | loop fusion | flops 19660800 | bytes 3292160 | tf_op jit(solution)/shard_map/convert_element_type | solution.py:49
  59.8 110.8 %all-to-all-done = bf16[16,40,5120]{2,1,0:T(8,128)(2,1)} async-done(((bf16[16,40,5120]{2,1,0:T(8,128)(2,1)}), bf16[16,40,5120]{2,1,0:T(8,128)(2,1)}, u32[]{:S(2)}, u32[]{:S(2)}) %all-to-all-start) | async-done | bytes 6553632 | tf_op jit(solution)/shard_map/all_to_all | solution.py:448
  170.7 13.0 %to_grid.1 = (f32[5,1280,512]{2,1,0:T(8,128)S(1)}, bf16[6400,128]{1,0:T(8,128)(2,1)S(1)}) custom-call(s32[3200]{0:T(1024)S(1)} %multiply_add_fusion.slots, bf16[2,640,640]{2,1,0:T(8,128)(2,1)S(1)} %get-tuple-element.11.table, bf16[640,5120]{1,0:T(8,128)(2,1)} %bitcast.2.coeffs), custom_call_target="tpu_custom_call" | custom-call | tf_op jit(solution)/shard_map/to_grid/pallas_call | solution.py:230
  183.7 4.7 copy-done.3
  188.3 42.5 %all_to_all.20 = bf16[16,400,128]{2,1,0:T(8,128)(2,1)S(1)} all-to-all(bf16[16,400,128]{2,1,0:T(8,128)(2,1)S(1)} %bitcast.30), channel_id=1, replica_groups=mesh['grp'=2,'wave'=16] {'wave'}, dimensions={0} | all-to-all | bytes 3276800 | tf_op jit(solution)/shard_map/all_to_all | solution.py:448
  230.9 23.2 %network.1 = bf16[6400,128]{1,0:T(8,128)(2,1)S(1)} custom-call(bf16[6400,128]{1,0:T(8,128)(2,1)S(1)} %bitcast.27, bf16[128,1024]{1,0:T(8,128)(2,1)S(1)} %bitcast.31, bf16[1024,1024]{1,0:T(8,128)(2,1)S(1)} %bitcast.29, bf16[1024,128]{1,0:T(8,128)(2,1)S(1)} %bitcast.32), custom_call_target="tpu_custom_call" | custom-call | tf_op jit(solution)/shard_map/network/pallas_call | solution.py:276
  254.2 42.6 %all_to_all.21 = bf16[16,400,128]{2,1,0:T(8,128)(2,1)S(1)} all-to-all(bf16[16,400,128]{2,1,0:T(8,128)(2,1)S(1)} %bitcast.28), channel_id=1, replica_groups=mesh['grp'=2,'wave'=16] {'wave'}, dimensions={0} | all-to-all | bytes 3276800 | tf_op jit(solution)/shard_map/all_to_all | solution.py:448
  296.8 4.7 copy-done.4
  301.5 13.6 %to_waves.1 = bf16[640,5120]{1,0:T(8,128)(2,1)S(1)} custom-call(s32[3200]{0:T(1024)S(1)} %multiply_add_fusion.slots, bf16[2,640,640]{2,1,0:T(8,128)(2,1)S(1)} %get-tuple-element.12.table, f32[5,1280,512]{2,1,0:T(8,128)S(1)} %copy-done.4, bf16[6400,128]{1,0:T(8,128)(2,1)S(1)} %bitcast.26), custom_call_target="tpu_custom_call" | custom-call | tf_op jit(solution)/shard_map/to_waves/pallas_call | solution.py:353
  315.2 2.8 copy-done.2
  317.9 6.7 %all-to-all-start.3 = ((bf16[16,40,5120]{2,1,0:T(8,128)(2,1)}), bf16[16,40,5120]{2,1,0:T(8,128)(2,1)}, u32[]{:S(2)}, u32[]{:S(2)}) async-start(bf16[16,40,5120]{2,1,0:T(8,128)(2,1)} %bitcast.25), calls=%async_computation.3 | async-start | bytes 13107200 | tf_op jit(solution)/shard_map/all_to_all | solution.py:448
  324.6 14.0 %copy.10.leg = bf16[20,641,320]{2,1,0:T(8,128)(2,1)} copy(bf16[20,641,320]{1,2,0:T(8,128)(2,1)} %param.9) | data formatting | bytes 16409600 | tf_op args[1]
  338.6 129.1 %all-to-all-done.3.coeffs = bf16[16,40,5120]{2,1,0:T(8,128)(2,1)} async-done(((bf16[16,40,5120]{2,1,0:T(8,128)(2,1)}), bf16[16,40,5120]{2,1,0:T(8,128)(2,1)}, u32[]{:S(2)}, u32[]{:S(2)}) %all-to-all-start.3) | async-done | bytes 6553632 | tf_op jit(solution)/shard_map/all_to_all | solution.py:448
  467.7 3.8 copy-done
  471.5 14.7 %forward_legendre.1 = bf16[20,641,256]{2,1,0:T(8,128)(2,1)} custom-call(s32[20]{0:T(128)S(1)} %dynamic_slice.3.low, bf16[16,40,5120]{2,1,0:T(8,128)(2,1)} %all-to-all-done.3.coeffs, bf16[20,641,320]{2,1,0:T(8,128)(2,1)S(1)} %copy-done, bf16[256,256]{1,0:T(8,128)(2,1)S(1)} %get-tuple-element.13.merge), custom_call_target="tpu_custom_call" | custom-call | tf_op jit(solution)/shard_map/forward_legendre/pallas_call | solution.py:430
  (33 shorter events, 0.8 us)
Async XLA Ops:
  0.9 2.9 copy-start.5
  18.2 2.8 copy-start.1
  21.0 6.7 %copy-start.10 = (s32[320]{0:T(512)S(1)}, s32[320]{0:T(512)}, u32[]{:S(2)}) copy-start(s32[320]{0:T(512)} %param.10) | copy-start | bytes 3844
  21.0 6.7 %copy-start.9 = (s32[3200,1]{0,1:T(1,128)S(1)}, s32[3200,1]{0,1:T(1,128)}, u32[]{:S(2)}) copy-start(s32[3200,1]{0,1:T(1,128)} %param.11) | copy-start | bytes 38404
  21.0 149.7 %all-to-all-start = ((bf16[16,40,5120]{2,1,0:T(8,128)(2,1)}), bf16[16,40,5120]{2,1,0:T(8,128)(2,1)}, u32[]{:S(2)}, u32[]{:S(2)}) async-start(bf16[16,40,5120]{2,1,0:T(8,128)(2,1)} %copy-done.1), calls=%async_computation | async-start | bytes 13107200 | tf_op jit(solution)/shard_map/all_to_all | solution.py:448
  183.7 4.7 copy-start.3
  188.3 42.6 %copy-start.6 = (bf16[1,1024,1024]{2,1,0:T(8,128)(2,1)S(1)}, bf16[1,1024,1024]{2,1,0:T(8,128)(2,1)}, u32[]{:S(2)}) copy-start(bf16[1,1024,1024]{2,1,0:T(8,128)(2,1)} %param.13) | copy-start | bytes 6291460
  188.3 42.6 %copy-start.7 = (bf16[1,128,1024]{2,1,0:T(8,128)(2,1)S(1)}, bf16[1,128,1024]{2,1,0:T(8,128)(2,1)}, u32[]{:S(2)}) copy-start(bf16[1,128,1024]{2,1,0:T(8,128)(2,1)} %param.12) | copy-start | bytes 786436
  188.3 42.6 %copy-start.8 = (bf16[1,1024,128]{2,1,0:T(8,128)(2,1)S(1)}, bf16[1,1024,128]{2,1,0:T(8,128)(2,1)}, u32[]{:S(2)}) copy-start(bf16[1,1024,128]{2,1,0:T(8,128)(2,1)} %param.14) | copy-start | bytes 786436
  296.8 4.7 copy-start.4
  315.1 2.8 copy-start.2
  317.9 149.7 %all-to-all-start.3 = ((bf16[16,40,5120]{2,1,0:T(8,128)(2,1)}), bf16[16,40,5120]{2,1,0:T(8,128)(2,1)}, u32[]{:S(2)}, u32[]{:S(2)}) async-start(bf16[16,40,5120]{2,1,0:T(8,128)(2,1)} %bitcast.25), calls=%async_computation.3 | async-start | bytes 13107200 | tf_op jit(solution)/shard_map/all_to_all | solution.py:448
  467.7 3.8 copy-start

commit v3 on v2

--- a/solution.py
+++ b/solution.py
@@ -1,4 +1,5 @@
 import functools
+import itertools
 import math
 
 import jax
@@ -12,10 +13,11 @@
 FIELDS = 4
 SPREAD = ((0.375, 0.625, 0.0), (0.125, 0.875, 0.0), (0.0, 0.875, 0.125), (0.0, 0.625, 0.375))
 PITCH_EXTRA = 8
-
-
-def params(mebibytes):
-    return pltpu.CompilerParams(vmem_limit_bytes=mebibytes * 1024 * 1024)
+VMEM_BYTES = 56 * 1024 * 1024
+
+
+def params():
+    return pltpu.CompilerParams(vmem_limit_bytes=VMEM_BYTES)
 
 
 def slot_positions(regimes, experts_total):
@@ -58,13 +60,6 @@
     return ((lat // together * 2 + parity) * together + lat % together) * feat
 
 
-def in_vmem(array):
-    return pltpu.with_memory_space_constraint(array, pltpu.VMEM)
-
-
-WHOLE = pl.BlockSpec(memory_space=pltpu.VMEM)
-
-
 def split_matrix(width):
     channel = jnp.arange(width, dtype=jnp.int32)
     target = (channel % 2) * (width // 2) + channel // 2
@@ -76,20 +71,23 @@
 
 
 def staggered(step, steps, first, second, slots):
+    def run(*parts):
+        for _ in itertools.zip_longest(*parts):
+            pass
+
     @pl.when(step == 0)
     def _():
-        first(0, slots[0])
+        run(first(0, slots[0]))
 
     for odd in range(2):
 
         @pl.when((step > 0) & (step < steps) & (step % 2 == odd))
         def _(odd=odd):
-            second(step - 1, slots[1 - odd])
-            first(step, slots[odd])
+            run(second(step - 1, slots[1 - odd]), first(step, slots[odd]))
 
     @pl.when(step == steps)
     def _():
-        second(steps - 1, slots[(steps - 1) % 2])
+        run(second(steps - 1, slots[(steps - 1) % 2]))
 
 
 def inverse_legendre_kernel(steps, low, spec, leg, split, out, *slots):
@@ -130,6 +128,7 @@
                     held[pl.ds(pl.multiple_of(start, 8), lat_total), :] = sides[s][
                         :, r * feat : (r + 1) * feat
                     ]
+            yield
 
     def turn(_, held):
         for d in range(devices):
@@ -139,6 +138,8 @@
                     own = held[pl.ds(start, rows, stride=pitch), :]
                     lane = lane_start(a, parity, lats, feat)
                     out[d, :, lane : lane + feat] = own.astype(jnp.bfloat16)
+            if (d + 1) % (devices // 4) == 0:
+                yield
 
     staggered(step, steps, transform, turn, slots)
 
@@ -164,7 +165,7 @@
         ),
         out_shape=jax.ShapeDtypeStruct((devices, 2 * pairs, lanes), jnp.bfloat16),
         scratch_shapes=[slot, slot],
-        compiler_params=params(40),
+        compiler_params=params(),
         name="inverse_legendre",
     )(local_low, spectral, legendre, split_matrix(channels))
 
@@ -172,19 +173,21 @@
 def to_grid_kernel(steps, slots, table, coeffs, forced, packed, cols, sent, *held):
     step = pl.program_id(0)
     count, feat = cols.shape
-    lanes = forced.shape[2]
+    lanes = forced.shape[1]
     half = table.shape[1]
     eighth = half // 4
     lat_rows = lanes // (2 * feat)
 
-    def transform(number, parts):
+    def transform(_, parts):
         for parity in range(2):
-            start = pl.multiple_of((2 * number + parity) * lanes, lanes)
-            parts[parity] = jnp.dot(
-                table[parity],
-                coeffs[:, pl.ds(start, lanes)],
-                preferred_element_type=jnp.float32,
-            )
+            for at in range(0, lanes, 2 * feat):
+                start = parity * lanes + at
+                parts[parity, :, at : at + 2 * feat] = jnp.dot(
+                    table[parity],
+                    coeffs[:, start : start + 2 * feat],
+                    preferred_element_type=jnp.float32,
+                )
+                yield
 
     def finish(number, parts):
         for i in range(lat_rows):
@@ -197,16 +200,18 @@
                     for h, field in enumerate((even + odd, even - odd)):
                         totals[h] = totals[h] + field
                         start = h * half + u * eighth
-                        forced[number, start : start + eighth, own] = field * pltpu.roll(
-                            field, feat - feat // FIELDS, axis=1
-                        )
+                        product = field * pltpu.roll(field, feat - feat // FIELDS, axis=1)
+                        forced[start : start + eighth, own] = product.astype(jnp.bfloat16)
+                if t == 2 * i:
+                    yield
             for h in range(2):
                 start = (2 * i + h) * eighth
                 cols[start : start + eighth, :] = (
                     (totals[h] * 0.125).astype(jnp.bfloat16).astype(jnp.float32)
                 )
-        for k in range(count):
-            sent[pl.ds(slots[number * count + k], 1), :] = cols[pl.ds(k, 1), :]
+            for k in range(2 * i * eighth, 2 * (i + 1) * eighth):
+                sent[pl.ds(slots[number * count + k], 1), :] = cols[pl.ds(k, 1), :]
+            yield
 
     @pl.when(step == 0)
     def _():
@@ -234,9 +239,12 @@
             grid=(steps + 1,),
             in_specs=[
                 pl.BlockSpec((2, NLON // 2, depth), lambda i, s: (0, 0, 0)),
-                WHOLE,
+                pl.BlockSpec((depth, 2 * own), lambda i, s: (0, jnp.minimum(i, steps - 1))),
             ],
-            out_specs=[WHOLE, pl.BlockSpec((slot_total, feat), lambda i, s: (0, 0))],
+            out_specs=[
+                pl.BlockSpec((NLON, own), lambda i, s: (0, jnp.maximum(i - 1, 0))),
+                pl.BlockSpec((slot_total, feat), lambda i, s: (0, 0)),
+            ],
             scratch_shapes=[
                 pltpu.VMEM((count, feat), jnp.float32),
                 pltpu.VMEM((slot_total, feat), jnp.float32),
@@ -245,12 +253,12 @@
             ],
         ),
         out_shape=[
-            pltpu.VMEM((steps, NLON, own), jnp.float32),
+            jax.ShapeDtypeStruct((NLON, lats * feat), jnp.bfloat16),
             jax.ShapeDtypeStruct((slot_total, feat), jnp.bfloat16),
         ],
-        compiler_params=params(30),
+        compiler_params=params(),
         name="to_grid",
-    )(slots, table, in_vmem(coeffs))
+    )(slots, table, coeffs)
 
 
 def silu(v):
@@ -284,7 +292,7 @@
         ],
         out_specs=pl.BlockSpec((block, feat), lambda i: (i, 0)),
         out_shape=jax.ShapeDtypeStruct((rows, feat), jnp.bfloat16),
-        compiler_params=params(30),
+        compiler_params=params(),
         name="network",
     )(columns, weight_in, weight_mid, weight_out)
 
@@ -292,17 +300,18 @@
 def to_waves_kernel(steps, slots, table, forced, answers, out, wide, *held):
     step = pl.program_id(0)
     count, feat = held[1].shape
-    lanes = forced.shape[2]
+    lanes = forced.shape[1]
     half = table.shape[2]
     eighth = half // 4
     quarter = 2 * eighth
 
-    def collect(number, cols):
-        for k in range(count):
+    def collect(number, cols, start, size):
+        for k in range(start, start + size):
             cols[pl.ds(k, 1), :] = wide[pl.ds(slots[number * count + k], 1), :]
 
     def fold(number, slot):
         folded, cols, next_cols = slot
+        after = jnp.minimum(number + 1, steps - 1)
         for i in range(count // quarter):
             coarse = cols[i * quarter : (i + 1) * quarter, :]
             before = pltpu.roll(coarse, 1, axis=0)
@@ -314,23 +323,31 @@
                 far_rows = slice(half + u * eighth, half + (u + 1) * eighth)
                 for t in (2 * i, 2 * i + 1):
                     own = slice(t * feat, (t + 1) * feat)
-                    near = forced[number, rows, own] + fine[:eighth]
-                    far = forced[number, far_rows, own] + fine[eighth:]
+                    near = forced[rows, own] + fine[:eighth]
+                    far = forced[far_rows, own] + fine[eighth:]
                     folded[0, rows, own] = (near + far).astype(jnp.bfloat16)
                     folded[1, rows, own] = (near - far).astype(jnp.bfloat16)
-        collect(jnp.minimum(number + 1, steps - 1), next_cols)
+                if u % 2 == 1:
+                    size = eighth
+                    collect(after, next_cols, (2 * i + u // 2) * size, size)
+                    yield
 
     def transform(_, slot):
         folded = slot[0]
         for parity in range(2):
-            out[:, parity * lanes : (parity + 1) * lanes] = jnp.dot(
-                table[parity], folded[parity], preferred_element_type=jnp.float32
-            ).astype(jnp.bfloat16)
+            for at in range(0, lanes, 2 * feat):
+                start = parity * lanes + at
+                out[:, start : start + 2 * feat] = jnp.dot(
+                    table[parity],
+                    folded[parity, :, at : at + 2 * feat],
+                    preferred_element_type=jnp.float32,
+                ).astype(jnp.bfloat16)
+                yield
 
     @pl.when(step == 0)
     def _():
         wide[...] = answers[...].astype(jnp.float32)
-        collect(0, held[1])
+        collect(0, held[1], 0, count)
 
     staggered(
         step,
@@ -342,10 +359,14 @@
 
 
 def to_waves(slots, table, forced, answers):
-    steps, _, own = forced.shape
+    lanes = forced.shape[1]
     slot_total, feat = answers.shape
     depth = table.shape[1]
-    count = own // feat // 2 * (NLON // 4)
+    lats = lanes // feat
+    together = lats_together(lats)
+    own = together * feat
+    count = together // 2 * (NLON // 4)
+    steps = lats // together
     slot = [
         pltpu.VMEM((2, NLON // 2, own), jnp.bfloat16),
         pltpu.VMEM((count, feat), jnp.float32),
@@ -357,7 +378,7 @@
             grid=(steps + 1,),
             in_specs=[
                 pl.BlockSpec((2, depth, NLON // 2), lambda i, s: (0, 0, 0)),
-                WHOLE,
+                pl.BlockSpec((NLON, own), lambda i, s: (0, jnp.minimum(i, steps - 1))),
                 pl.BlockSpec((slot_total, feat), lambda i, s: (0, 0)),
             ],
             out_specs=pl.BlockSpec((depth, 2 * own), lambda i, s: (0, jnp.maximum(i - 1, 0))),
@@ -367,10 +388,10 @@
                 *slot,
             ],
         ),
-        out_shape=jax.ShapeDtypeStruct((depth, 2 * steps * own), jnp.bfloat16),
-        compiler_params=params(30),
+        out_shape=jax.ShapeDtypeStruct((depth, 2 * lanes), jnp.bfloat16),
+        compiler_params=params(),
         name="to_waves",
-    )(slots, table, in_vmem(forced), answers)
+    )(slots, table, forced, answers)
 
 
 def forward_legendre_kernel(steps, low, coeffs, leg, merge, out, *slots):
@@ -378,23 +399,22 @@
     group, degrees, channels = out.shape
     feat = channels // 2
     lat_total = leg.shape[2]
-    devices, rows = coeffs.shape[0], 2 * group
+    devices, rows = coeffs.shape[:2]
     lats = lat_total // devices
     pitch = lat_total + PITCH_EXTRA
     middle = (degrees - 1) // 2
 
-    def turn(number, held):
-        own_rows = slice(None)
-        if coeffs.shape[1] > rows:
-            own_rows = pl.ds(pl.multiple_of(number * rows, rows), rows)
+    def turn(_, held):
         for d in range(devices):
             for a in range(lats):
                 for parity in range(2):
                     start = parity * rows * pitch + d * lats + a
                     lane = lane_start(a, parity, lats, feat)
                     held[pl.ds(start, rows, stride=pitch), :] = coeffs[
-                        d, own_rows, lane : lane + feat
+                        d, :, lane : lane + feat
                     ].astype(jnp.float32)
+            if (d + 1) % (devices // 4) == 0:
+                yield
 
     def transform(number, held):
         for g in range(group):
@@ -408,8 +428,8 @@
                     start = (parity * rows + 2 * g + r) * pitch
                     parts.append(held[pl.ds(pl.multiple_of(start, 8), lat_total), :])
                 sides.append(jnp.concatenate(parts, axis=1).astype(jnp.bfloat16))
-            first = jnp.dot(leg[number * group + g], sides[0], preferred_element_type=jnp.float32)
-            second = jnp.dot(leg[number * group + g, middle:], sides[1], preferred_element_type=jnp.float32)
+            first = jnp.dot(leg[g], sides[0], preferred_element_type=jnp.float32)
+            second = jnp.dot(leg[g, middle:], sides[1], preferred_element_type=jnp.float32)
             on_first = lax.broadcasted_iota(jnp.int32, second.shape, 0) < lower - middle
             chosen = jnp.concatenate(
                 [first[:middle], jnp.where(on_first, first[middle:], second)], axis=0
@@ -417,6 +437,7 @@
             out[g] = jnp.dot(
                 chosen.astype(jnp.bfloat16), merge[...], preferred_element_type=jnp.float32
             ).astype(jnp.bfloat16)
+            yield
 
     staggered(step, steps, turn, transform, slots)
 
@@ -432,16 +453,18 @@
         grid=(steps + 1,),
         in_specs=[
             pl.BlockSpec(memory_space=pltpu.SMEM),
-            WHOLE,
-            WHOLE,
+            pl.BlockSpec(
+                (devices, 2 * group, lanes), lambda i: (0, jnp.minimum(i, steps - 1), 0)
+            ),
+            pl.BlockSpec((group, degrees, lat_total), lambda i: (jnp.maximum(i - 1, 0), 0, 0)),
             pl.BlockSpec((channels, channels), lambda i: (0, 0)),
         ],
         out_specs=pl.BlockSpec((group, degrees, channels), lambda i: (jnp.maximum(i - 1, 0), 0, 0)),
         out_shape=jax.ShapeDtypeStruct((pairs, degrees, channels), jnp.bfloat16),
         scratch_shapes=[slot, slot],
-        compiler_params=params(30),
+        compiler_params=params(),
         name="forward_legendre",
-    )(local_low, in_vmem(coeffs), in_vmem(legendre), split_matrix(channels).T)
+    )(local_low, coeffs, legendre, split_matrix(channels).T)
 
 
 def exchange(blocks):

time: 487 us -> 472 us (0.969)
  local copies, waits for them, and re-layouts: 37.4 us -> 16.3 us
    unnamed x23 -> x5, local copies, waits for them, and re-layouts: 35.6 us -> 14 us
  transfers between devices with their start and end apart: 2 -> 2, of which waited for: 2 -> 2; matrix products, arithmetic and copies ran while one was open for 9% -> 10% of each run, Pallas kernels for 0% -> 0%
where the time goes in v3:
time: 472 us; the launch traced here: 471 us
  waiting for transfers between devices  238 us (50%)
  blocking collectives  86.7 us (18%)
  Pallas kernels  82.9 us (18%)
  other arithmetic  33.5 us (7%)
  local copies, waits for them, and re-layouts  16.3 us (3%)
  starting transfers between devices  13.4 us (3%)
    all_to_all x2, waiting for transfers between devices, exchange(): lax.all_to_all(blocks, 'wave', split_axis=0, concat_axis=0, tiled=True)  238 us
    all_to_all x2, blocking collectives, exchange(): lax.all_to_all(blocks, 'wave', split_axis=0, concat_axis=0, tiled=True)  86.7 us
    convert_element_type x1, other arithmetic, zonal_tables(): return (inverse.astype(jnp.bfloat16), forward.astype(jnp.bfloat16))  26.9 us
    pallas_call x1, Pallas kernels, network(): pl.pallas_call(network_kernel, grid=(rows // block,), in_specs=[pl.BlockS...  25.5 us
    pallas_call x1, Pallas kernels, inverse_legendre(): pl.pallas_call(functools.partial(inverse_legendre_kernel, steps), grid=(s...  14.9 us
    pallas_call x1, Pallas kernels, to_waves(): pl.pallas_call(functools.partial(to_waves_kernel, steps), grid_spec=pltpu...  14.4 us
    pallas_call x1, Pallas kernels, to_grid(): pl.pallas_call(functools.partial(to_grid_kernel, steps), grid_spec=pltpu....  14.1 us
    unnamed x5, local copies, waits for them, and re-layouts  14 us
  transfers between devices with their start and end apart: 2, of which 2 were waited for; matrix products, arithmetic and copies ran while one was open for 10% of the time, Pallas kernels for 0%

profile of v3, /device:TPU:13, one launch (start us, length us, event | category | flops | bytes accessed | tf_op | source)
XLA Modules:
  0.0 471.2 jit_solution(13225939372081714954)
XLA Ops:
  0.0 0.7 fusion.18
  0.8 1.3 dynamic_slice.3.low
  2.0 14.9 %inverse_legendre.1 = bf16[16,40,5120]{2,1,0:T(8,128)(2,1)} custom-call(s32[20]{0:T(128)} %dynamic_slice.3.low, bf16[20,641,256]{2,1,0:T(8,128)(2,1)} %spec.1, bf16[20,320,641]{2,1,0:T(8,128)(2,1)} %bitcast.25, bf16[256,256]{1,0:T(8,128)(2,1)} %get-tuple-element.14.split), custom_call_target="tpu_custom_call" | custom-call | tf_op jit(solution)/shard_map/inverse_legendre/pallas_call | solution.py:154
  16.9 6.7 %all-to-all-start = ((bf16[16,40,5120]{2,1,0:T(8,128)(2,1)}), bf16[16,40,5120]{2,1,0:T(8,128)(2,1)}, u32[]{:S(2)}, u32[]{:S(2)}) async-start(bf16[16,40,5120]{2,1,0:T(8,128)(2,1)} %inverse_legendre.1), calls=%async_computation | async-start | bytes 13107200 | tf_op jit(solution)/shard_map/all_to_all | solution.py:471
  23.8 0.1 broadcast_in_dim.16
  23.9 4.6 reduce-window.6
  28.6 0.5 slice_reduce_fusion
  29.0 0.2 reduce-window.9
  29.2 0.1 broadcast_in_dim.14
  29.4 0.2 mul.90
  29.6 0.1 add_add_fusion
  29.8 0.1 fusion.20
  29.9 0.6 multiply_add_fusion.slots
  30.5 26.9 %fusion.9 = (bf16[2,640,640]{2,1,0:T(8,128)(2,1)}, bf16[2,640,640]{2,1,0:T(8,128)(2,1)}) fusion(s32[640]{0:T(1024)S(1)} %broadcast_in_dim.16, s32[640]{0:T(1024)S(1)} %fusion.27, s32[2,640]{1,0:T(2,128)S(1)} %mul.90, f32[2,640]{1,0:T(2,128)S(1)} %compare_select_fusion), kind=kLoop, calls=%fused_computation.11 | loop fusion | flops 19660800 | bytes 3292160 | tf_op jit(solution)/shard_map/convert_element_type | solution.py:51
  57.5 109.2 %all-to-all-done = bf16[16,40,5120]{2,1,0:T(8,128)(2,1)} async-done(((bf16[16,40,5120]{2,1,0:T(8,128)(2,1)}), bf16[16,40,5120]{2,1,0:T(8,128)(2,1)}, u32[]{:S(2)}, u32[]{:S(2)}) %all-to-all-start) | async-done | bytes 6553632 | tf_op jit(solution)/shard_map/all_to_all | solution.py:471
  166.7 14.1 %to_grid.1 = (bf16[1280,2560]{1,0:T(8,128)(2,1)}, bf16[6400,128]{1,0:T(8,128)(2,1)}) custom-call(s32[3200]{0:T(1024)} %multiply_add_fusion.slots, bf16[2,640,640]{2,1,0:T(8,128)(2,1)} %get-tuple-element.11.table, bf16[640,5120]{1,0:T(8,128)(2,1)} %bitcast.2.coeffs), custom_call_target="tpu_custom_call" | custom-call | tf_op jit(solution)/shard_map/to_grid/pallas_call | solution.py:235
  180.8 42.6 %all_to_all.20 = bf16[16,400,128]{2,1,0:T(8,128)(2,1)} all-to-all(bf16[16,400,128]{2,1,0:T(8,128)(2,1)} %bitcast.31), channel_id=1, replica_groups=mesh['grp'=2,'wave'=16] {'wave'}, dimensions={0} | all-to-all | bytes 3276800 | tf_op jit(solution)/shard_map/all_to_all | solution.py:471
  223.4 25.5 %network.1 = bf16[6400,128]{1,0:T(8,128)(2,1)} custom-call(bf16[6400,128]{1,0:T(8,128)(2,1)} %bitcast.28, bf16[128,1024]{1,0:T(8,128)(2,1)} %bitcast.33, bf16[1024,1024]{1,0:T(8,128)(2,1)} %bitcast.30, bf16[1024,128]{1,0:T(8,128)(2,1)} %bitcast.34), custom_call_target="tpu_custom_call" | custom-call | tf_op jit(solution)/shard_map/network/pallas_call | solution.py:284
  248.9 44.1 %all_to_all.21 = bf16[16,400,128]{2,1,0:T(8,128)(2,1)} all-to-all(bf16[16,400,128]{2,1,0:T(8,128)(2,1)} %bitcast.29), channel_id=1, replica_groups=mesh['grp'=2,'wave'=16] {'wave'}, dimensions={0} | all-to-all | bytes 3276800 | tf_op jit(solution)/shard_map/all_to_all | solution.py:471
  293.0 14.4 %to_waves.1 = bf16[640,5120]{1,0:T(8,128)(2,1)} custom-call(s32[3200]{0:T(1024)} %multiply_add_fusion.slots, bf16[2,640,640]{2,1,0:T(8,128)(2,1)} %get-tuple-element.12.table, bf16[1280,2560]{1,0:T(8,128)(2,1)} %get-tuple-element.7.forced, bf16[6400,128]{1,0:T(8,128)(2,1)} %bitcast.27), custom_call_target="tpu_custom_call" | custom-call | tf_op jit(solution)/shard_map/to_waves/pallas_call | solution.py:374
  307.4 6.7 %all-to-all-start.3 = ((bf16[16,40,5120]{2,1,0:T(8,128)(2,1)}), bf16[16,40,5120]{2,1,0:T(8,128)(2,1)}, u32[]{:S(2)}, u32[]{:S(2)}) async-start(bf16[16,40,5120]{2,1,0:T(8,128)(2,1)} %bitcast.26), calls=%async_computation.3 | async-start | bytes 13107200 | tf_op jit(solution)/shard_map/all_to_all | solution.py:471
  314.1 14.0 %copy.10.leg = bf16[20,641,320]{2,1,0:T(8,128)(2,1)} copy(bf16[20,641,320]{1,2,0:T(8,128)(2,1)} %param.9) | data formatting | bytes 16409600 | tf_op args[1]
  328.1 129.0 %all-to-all-done.3.coeffs = bf16[16,40,5120]{2,1,0:T(8,128)(2,1)} async-done(((bf16[16,40,5120]{2,1,0:T(8,128)(2,1)}), bf16[16,40,5120]{2,1,0:T(8,128)(2,1)}, u32[]{:S(2)}, u32[]{:S(2)}) %all-to-all-start.3) | async-done | bytes 6553632 | tf_op jit(solution)/shard_map/all_to_all | solution.py:471
  457.1 14.0 %forward_legendre.1 = bf16[20,641,256]{2,1,0:T(8,128)(2,1)} custom-call(s32[20]{0:T(128)} %dynamic_slice.3.low, bf16[16,40,5120]{2,1,0:T(8,128)(2,1)} %all-to-all-done.3.coeffs, bf16[20,641,320]{2,1,0:T(8,128)(2,1)} %copy.10.leg, bf16[256,256]{1,0:T(8,128)(2,1)} %get-tuple-element.13.merge), custom_call_target="tpu_custom_call" | custom-call | tf_op jit(solution)/shard_map/forward_legendre/pallas_call | solution.py:451
  (15 shorter events, 0.1 us)
Async XLA Ops:
  16.9 6.7 %copy-start.1 = (s32[320]{0:T(512)S(1)}, s32[320]{0:T(512)}, u32[]{:S(2)}) copy-start(s32[320]{0:T(512)} %param.10) | copy-start | bytes 3844
  16.9 6.7 %copy-start = (s32[3200,1]{0,1:T(1,128)S(1)}, s32[3200,1]{0,1:T(1,128)}, u32[]{:S(2)}) copy-start(s32[3200,1]{0,1:T(1,128)} %param.11) | copy-start | bytes 38404
  16.9 149.7 %all-to-all-start = ((bf16[16,40,5120]{2,1,0:T(8,128)(2,1)}), bf16[16,40,5120]{2,1,0:T(8,128)(2,1)}, u32[]{:S(2)}, u32[]{:S(2)}) async-start(bf16[16,40,5120]{2,1,0:T(8,128)(2,1)} %inverse_legendre.1), calls=%async_computation | async-start | bytes 13107200 | tf_op jit(solution)/shard_map/all_to_all | solution.py:471
  307.4 149.7 %all-to-all-start.3 = ((bf16[16,40,5120]{2,1,0:T(8,128)(2,1)}), bf16[16,40,5120]{2,1,0:T(8,128)(2,1)}, u32[]{:S(2)}, u32[]{:S(2)}) async-start(bf16[16,40,5120]{2,1,0:T(8,128)(2,1)} %bitcast.26), calls=%async_computation.3 | async-start | bytes 13107200 | tf_op jit(solution)/shard_map/all_to_all | solution.py:471

commit v4 on v3

--- a/solution.py
+++ b/solution.py
@@ -4,6 +4,7 @@
 
 import jax
 import jax.numpy as jnp
+import numpy as np
 from jax import lax
 from jax.experimental import pallas as pl
 from jax.experimental.pallas import tpu as pltpu
@@ -13,11 +14,14 @@
 FIELDS = 4
 SPREAD = ((0.375, 0.625, 0.0), (0.125, 0.875, 0.0), (0.0, 0.875, 0.125), (0.0, 0.625, 0.375))
 PITCH_EXTRA = 8
-VMEM_BYTES = 56 * 1024 * 1024
-
-
-def params():
-    return pltpu.CompilerParams(vmem_limit_bytes=VMEM_BYTES)
+
+
+def params(mebibytes):
+    return pltpu.CompilerParams(vmem_limit_bytes=mebibytes * 1024 * 1024)
+
+
+def in_hbm(array):
+    return pltpu.with_memory_space_constraint(array, pltpu.HBM)
 
 
 def slot_positions(regimes, experts_total):
@@ -61,7 +65,7 @@
 
 
 def split_matrix(width):
-    channel = jnp.arange(width, dtype=jnp.int32)
+    channel = np.arange(width)
     target = (channel % 2) * (width // 2) + channel // 2
     return (target[:, None] == channel[None, :]).astype(jnp.bfloat16)
 
@@ -101,9 +105,11 @@
     middle = (degrees - 1) // 2
     skip = middle // 256 * 256
 
+    first_pair = lax.axis_index("wave") * steps * group
+
     def transform(number, held):
         for g in range(group):
-            own_low = low[number * group + g]
+            own_low = low[first_pair + number * group + g]
             lower = degrees - 1 - own_low
             coeffs = jnp.dot(spec[g], split[...], preferred_element_type=jnp.float32)
             tail = coeffs[middle:]
@@ -144,7 +150,7 @@
     staggered(step, steps, transform, turn, slots)
 
 
-def inverse_legendre(spectral, legendre, local_low, devices):
+def inverse_legendre(spectral, legendre, pair_low, devices):
     pairs, degrees, channels = spectral.shape
     lat_total = legendre.shape[1]
     lanes = lat_total // devices * channels
@@ -163,11 +169,11 @@
         out_specs=pl.BlockSpec(
             (devices, 2 * group, lanes), lambda i: (0, jnp.maximum(i - 1, 0), 0)
         ),
-        out_shape=jax.ShapeDtypeStruct((devices, 2 * pairs, lanes), jnp.bfloat16),
+        out_shape=pltpu.HBM((devices, 2 * pairs, lanes), jnp.bfloat16),
         scratch_shapes=[slot, slot],
-        compiler_params=params(),
+        compiler_params=params(56),
         name="inverse_legendre",
-    )(local_low, spectral, legendre, split_matrix(channels))
+    )(pair_low, in_hbm(spectral), in_hbm(legendre), split_matrix(channels))
 
 
 def to_grid_kernel(steps, slots, table, coeffs, forced, packed, cols, sent, *held):
@@ -253,12 +259,12 @@
             ],
         ),
         out_shape=[
-            jax.ShapeDtypeStruct((NLON, lats * feat), jnp.bfloat16),
+            pltpu.HBM((NLON, lats * feat), jnp.bfloat16),
             jax.ShapeDtypeStruct((slot_total, feat), jnp.bfloat16),
         ],
-        compiler_params=params(),
+        compiler_params=params(36),
         name="to_grid",
-    )(slots, table, coeffs)
+    )(slots, table, in_hbm(coeffs))
 
 
 def silu(v):
@@ -292,7 +298,7 @@
         ],
         out_specs=pl.BlockSpec((block, feat), lambda i: (i, 0)),
         out_shape=jax.ShapeDtypeStruct((rows, feat), jnp.bfloat16),
-        compiler_params=params(),
+        compiler_params=params(36),
         name="network",
     )(columns, weight_in, weight_mid, weight_out)
 
@@ -388,10 +394,10 @@
                 *slot,
             ],
         ),
-        out_shape=jax.ShapeDtypeStruct((depth, 2 * lanes), jnp.bfloat16),
-        compiler_params=params(),
+        out_shape=pltpu.HBM((depth, 2 * lanes), jnp.bfloat16),
+        compiler_params=params(36),
         name="to_waves",
-    )(slots, table, forced, answers)
+    )(slots, table, in_hbm(forced), answers)
 
 
 def forward_legendre_kernel(steps, low, coeffs, leg, merge, out, *slots):
@@ -416,9 +422,11 @@
             if (d + 1) % (devices // 4) == 0:
                 yield
 
+    first_pair = lax.axis_index("wave") * steps * group
+
     def transform(number, held):
         for g in range(group):
-            own_low = low[number * group + g]
+            own_low = low[first_pair + number * group + g]
             lower = degrees - 1 - own_low
             sides = []
             for s in range(2):
@@ -442,7 +450,7 @@
     staggered(step, steps, turn, transform, slots)
 
 
-def forward_legendre(coeffs, legendre, local_low, channels):
+def forward_legendre(coeffs, legendre, pair_low, channels):
     devices, rows, lanes = coeffs.shape
     pairs, degrees, lat_total = legendre.shape
     group = group_of(pairs)
@@ -462,9 +470,9 @@
         out_specs=pl.BlockSpec((group, degrees, channels), lambda i: (jnp.maximum(i - 1, 0), 0, 0)),
         out_shape=jax.ShapeDtypeStruct((pairs, degrees, channels), jnp.bfloat16),
         scratch_shapes=[slot, slot],
-        compiler_params=params(),
+        compiler_params=params(56),
         name="forward_legendre",
-    )(local_low, coeffs, legendre, split_matrix(channels).T)
+    )(pair_low, in_hbm(coeffs), in_hbm(legendre), split_matrix(channels).T)
 
 
 def exchange(blocks):
@@ -472,12 +480,10 @@
 
 
 def on_device(spectral, legendre, pair_low, routes, w_in, w_mid, w_out):
-    pairs, degrees, channels = spectral.shape
+    _, degrees, channels = spectral.shape
     feat = channels // 2
     devices = lax.axis_size("wave")
-    local_low = lax.dynamic_slice_in_dim(pair_low, lax.axis_index("wave") * pairs, pairs)
-
-    sent = inverse_legendre(spectral, jnp.swapaxes(legendre, 1, 2), local_low, devices)
+    sent = inverse_legendre(spectral, jnp.swapaxes(legendre, 1, 2), pair_low, devices)
     arrived = exchange(sent)
     inverse_table, forward_table = zonal_tables(pair_low, degrees - 1)
     regimes = routes[:, 0]
@@ -492,7 +498,7 @@
     incoming = exchange(answers.reshape(devices, capacity, feat)).reshape(-1, feat)
     waves = to_waves(slots, forward_table, forced, incoming)
     received = exchange(waves.reshape(arrived.shape))
-    return forward_legendre(received, legendre, local_low, channels)
+    return forward_legendre(received, legendre, pair_low, channels)
 
 
 def solution(mesh):

time: 472 us -> 464 us (0.983)
    unnamed x5 -> x11, local copies, waits for them, and re-layouts: 14 us -> 14 us
where the time goes in v4:
time: 464 us; the launch traced here: 463 us
  waiting for transfers between devices  240 us (52%)
  blocking collectives  85.2 us (18%)
  Pallas kernels  78.2 us (17%)
  other arithmetic  31.1 us (7%)
  local copies, waits for them, and re-layouts  15 us (3%)
  starting transfers between devices  13.4 us (3%)
    all_to_all x2, waiting for transfers between devices, exchange(): lax.all_to_all(blocks, 'wave', split_axis=0, concat_axis=0, tiled=True)  240 us
    all_to_all x2, blocking collectives, exchange(): lax.all_to_all(blocks, 'wave', split_axis=0, concat_axis=0, tiled=True)  85.2 us
    convert_element_type x1, other arithmetic, zonal_tables(): return (inverse.astype(jnp.bfloat16), forward.astype(jnp.bfloat16))  25.9 us
    pallas_call x1, Pallas kernels, network(): pl.pallas_call(network_kernel, grid=(rows // block,), in_specs=[pl.BlockS...  22.9 us
    pallas_call x1, Pallas kernels, inverse_legendre(): pl.pallas_call(functools.partial(inverse_legendre_kernel, steps), grid=(s...  14.9 us
    unnamed x11, local copies, waits for them, and re-layouts  14 us
    pallas_call x1, Pallas kernels, forward_legendre(): pl.pallas_call(functools.partial(forward_legendre_kernel, steps), grid=(s...  14 us
    all_to_all x2, starting transfers between devices, exchange(): lax.all_to_all(blocks, 'wave', split_axis=0, concat_axis=0, tiled=True)  13.4 us
  transfers between devices with their start and end apart: 2, of which 2 were waited for; matrix products, arithmetic and copies ran while one was open for 10% of the time, Pallas kernels for 0%

profile of v4, /device:TPU:13, one launch (start us, length us, event | category | flops | bytes accessed | tf_op | source)
XLA Modules:
  0.0 462.9 jit_solution(1464681670046284970)
XLA Ops:
  0.0 14.9 %inverse_legendre.1 = bf16[16,40,5120]{2,1,0:T(8,128)(2,1)} custom-call(s32[320]{0:T(512)} %low.3, bf16[20,641,256]{2,1,0:T(8,128)(2,1)} %spec.1, bf16[20,320,641]{2,1,0:T(8,128)(2,1)} %bitcast.32, bf16[256,256]{1,0:T(8,128)(2,1)} %constant.77.clone.split), custom_call_target="tpu_custom_call" | custom-call | tf_op jit(solution)/shard_map/inverse_legendre/pallas_call | solution.py:160
  14.9 6.7 %all-to-all-start = ((bf16[16,40,5120]{2,1,0:T(8,128)(2,1)}), bf16[16,40,5120]{2,1,0:T(8,128)(2,1)}, u32[]{:S(2)}, u32[]{:S(2)}) async-start(bf16[16,40,5120]{2,1,0:T(8,128)(2,1)} %inverse_legendre.1), calls=%async_computation | async-start | bytes 13107200 | tf_op jit(solution)/shard_map/all_to_all | solution.py:479
  21.6 0.0 copy-done.3
  21.7 0.1 broadcast_in_dim.26
  21.8 0.0 copy-done.4
  21.9 4.6 reduce-window.6
  26.5 0.5 slice_reduce_fusion
  27.0 0.2 reduce-window.9
  27.2 0.1 broadcast_in_dim.24
  27.3 0.2 mul.76
  27.6 0.1 add_add_fusion
  27.7 0.1 fusion.18
  27.9 25.9 %fusion.9 = (bf16[2,640,640]{2,1,0:T(8,128)(2,1)S(1)}, bf16[2,640,640]{2,1,0:T(8,128)(2,1)S(1)}) fusion(s32[640]{0:T(1024)S(1)} %broadcast_in_dim.26, s32[640]{0:T(1024)S(1)} %fusion.25, s32[2,640]{1,0:T(2,128)S(1)} %mul.76, f32[2,640]{1,0:T(2,128)S(1)} %compare_select_fusion), kind=kLoop, calls=%fused_computation.11 | loop fusion | flops 19660800 | bytes 3292160 | tf_op jit(solution)/shard_map/convert_element_type | solution.py:55
  53.8 110.8 %all-to-all-done = bf16[16,40,5120]{2,1,0:T(8,128)(2,1)} async-done(((bf16[16,40,5120]{2,1,0:T(8,128)(2,1)}), bf16[16,40,5120]{2,1,0:T(8,128)(2,1)}, u32[]{:S(2)}, u32[]{:S(2)}) %all-to-all-start) | async-done | bytes 6553632 | tf_op jit(solution)/shard_map/all_to_all | solution.py:479
  164.6 13.1 %to_grid.1 = (bf16[1280,2560]{1,0:T(8,128)(2,1)}, bf16[6400,128]{1,0:T(8,128)(2,1)S(1)}) custom-call(s32[3200]{0:T(1024)S(1)} %multiply_add_fusion.slots, bf16[2,640,640]{2,1,0:T(8,128)(2,1)S(1)} %get-tuple-element.11.table, bf16[640,5120]{1,0:T(8,128)(2,1)} %bitcast.2.coeffs), custom_call_target="tpu_custom_call" | custom-call | tf_op jit(solution)/shard_map/to_grid/pallas_call | solution.py:241
  177.7 42.6 %all_to_all.20 = bf16[16,400,128]{2,1,0:T(8,128)(2,1)S(1)} all-to-all(bf16[16,400,128]{2,1,0:T(8,128)(2,1)S(1)} %bitcast.29), channel_id=1, replica_groups=mesh['grp'=2,'wave'=16] {'wave'}, dimensions={0} | all-to-all | bytes 3276800 | tf_op jit(solution)/shard_map/all_to_all | solution.py:479
  220.3 0.0 copy-done.1
  220.3 22.9 %network.1 = bf16[6400,128]{1,0:T(8,128)(2,1)S(1)} custom-call(bf16[6400,128]{1,0:T(8,128)(2,1)S(1)} %bitcast.26, bf16[128,1024]{1,0:T(8,128)(2,1)S(1)} %bitcast.30, bf16[1024,1024]{1,0:T(8,128)(2,1)S(1)} %bitcast.28, bf16[1024,128]{1,0:T(8,128)(2,1)S(1)} %bitcast.31), custom_call_target="tpu_custom_call" | custom-call | tf_op jit(solution)/shard_map/network/pallas_call | solution.py:290
  243.3 42.6 %all_to_all.21 = bf16[16,400,128]{2,1,0:T(8,128)(2,1)S(1)} all-to-all(bf16[16,400,128]{2,1,0:T(8,128)(2,1)S(1)} %bitcast.27), channel_id=1, replica_groups=mesh['grp'=2,'wave'=16] {'wave'}, dimensions={0} | all-to-all | bytes 3276800 | tf_op jit(solution)/shard_map/all_to_all | solution.py:479
  285.9 13.2 %to_waves.1 = bf16[640,5120]{1,0:T(8,128)(2,1)} custom-call(s32[3200]{0:T(1024)S(1)} %multiply_add_fusion.slots, bf16[2,640,640]{2,1,0:T(8,128)(2,1)S(1)} %get-tuple-element.12.table, bf16[1280,2560]{1,0:T(8,128)(2,1)} %get-tuple-element.7.forced, bf16[6400,128]{1,0:T(8,128)(2,1)S(1)} %bitcast.25), custom_call_target="tpu_custom_call" | custom-call | tf_op jit(solution)/shard_map/to_waves/pallas_call | solution.py:380
  299.1 6.7 %all-to-all-start.3 = ((bf16[16,40,5120]{2,1,0:T(8,128)(2,1)}), bf16[16,40,5120]{2,1,0:T(8,128)(2,1)}, u32[]{:S(2)}, u32[]{:S(2)}) async-start(bf16[16,40,5120]{2,1,0:T(8,128)(2,1)} %bitcast.33), calls=%async_computation.3 | async-start | bytes 13107200 | tf_op jit(solution)/shard_map/all_to_all | solution.py:479
  305.8 14.0 %copy.12.leg = bf16[20,641,320]{2,1,0:T(8,128)(2,1)} copy(bf16[20,641,320]{1,2,0:T(8,128)(2,1)} %param.11) | data formatting | bytes 16409600 | tf_op args[1]
  319.8 129.0 %all-to-all-done.3.coeffs = bf16[16,40,5120]{2,1,0:T(8,128)(2,1)} async-done(((bf16[16,40,5120]{2,1,0:T(8,128)(2,1)}), bf16[16,40,5120]{2,1,0:T(8,128)(2,1)}, u32[]{:S(2)}, u32[]{:S(2)}) %all-to-all-start.3) | async-done | bytes 6553632 | tf_op jit(solution)/shard_map/all_to_all | solution.py:479
  448.8 14.0 %forward_legendre.1 = bf16[20,641,256]{2,1,0:T(8,128)(2,1)} custom-call(s32[320]{0:T(512)} %low.3, bf16[16,40,5120]{2,1,0:T(8,128)(2,1)} %all-to-all-done.3.coeffs, bf16[20,641,320]{2,1,0:T(8,128)(2,1)} %copy.12.leg, bf16[256,256]{1,0:T(8,128)(2,1)} %constant.79.clone.merge), custom_call_target="tpu_custom_call" | custom-call | tf_op jit(solution)/shard_map/forward_legendre/pallas_call | solution.py:459
  (18 shorter events, 0.1 us)
Async XLA Ops:
  14.9 6.7 %copy-start.3 = (s32[320]{0:T(512)S(1)}, s32[320]{0:T(512)}, u32[]{:S(2)}) copy-start(s32[320]{0:T(512)} %low.3) | copy-start | bytes 3844
  14.9 6.9 %copy-start.4 = (s32[3200,1]{0,1:T(1,128)S(1)}, s32[3200,1]{0,1:T(1,128)}, u32[]{:S(2)}) copy-start(s32[3200,1]{0,1:T(1,128)} %param.13) | copy-start | bytes 38404
  14.9 149.7 %all-to-all-start = ((bf16[16,40,5120]{2,1,0:T(8,128)(2,1)}), bf16[16,40,5120]{2,1,0:T(8,128)(2,1)}, u32[]{:S(2)}, u32[]{:S(2)}) async-start(bf16[16,40,5120]{2,1,0:T(8,128)(2,1)} %inverse_legendre.1), calls=%async_computation | async-start | bytes 13107200 | tf_op jit(solution)/shard_map/all_to_all | solution.py:479
  177.7 42.6 %copy-start = (bf16[1,1024,1024]{2,1,0:T(8,128)(2,1)S(1)}, bf16[1,1024,1024]{2,1,0:T(8,128)(2,1)}, u32[]{:S(2)}) copy-start(bf16[1,1024,1024]{2,1,0:T(8,128)(2,1)} %param.15) | copy-start | bytes 6291460
  177.7 42.6 %copy-start.1 = (bf16[1,128,1024]{2,1,0:T(8,128)(2,1)S(1)}, bf16[1,128,1024]{2,1,0:T(8,128)(2,1)}, u32[]{:S(2)}) copy-start(bf16[1,128,1024]{2,1,0:T(8,128)(2,1)} %param.14) | copy-start | bytes 786436
  177.7 42.6 %copy-start.2 = (bf16[1,1024,128]{2,1,0:T(8,128)(2,1)S(1)}, bf16[1,1024,128]{2,1,0:T(8,128)(2,1)}, u32[]{:S(2)}) copy-start(bf16[1,1024,128]{2,1,0:T(8,128)(2,1)} %param.16) | copy-start | bytes 786436
  299.1 149.7 %all-to-all-start.3 = ((bf16[16,40,5120]{2,1,0:T(8,128)(2,1)}), bf16[16,40,5120]{2,1,0:T(8,128)(2,1)}, u32[]{:S(2)}, u32[]{:S(2)}) async-start(bf16[16,40,5120]{2,1,0:T(8,128)(2,1)} %bitcast.33), calls=%async_computation.3 | async-start | bytes 13107200 | tf_op jit(solution)/shard_map/all_to_all | solution.py:479

commit v5 on v4

--- a/solution.py
+++ b/solution.py
@@ -107,25 +107,28 @@
 
     first_pair = lax.axis_index("wave") * steps * group
 
+    def prepare(number, g):
+        own_low = low[first_pair + number * group + g]
+        lower = degrees - 1 - own_low
+        coeffs = jnp.dot(spec[g], split[...], preferred_element_type=jnp.float32)
+        tail = coeffs[middle:]
+        on_first = lax.broadcasted_iota(jnp.int32, tail.shape, 0) < lower - middle
+        first = jnp.concatenate([coeffs[:middle], jnp.where(on_first, tail, 0.0)], axis=0)
+        second = jnp.concatenate(
+            [jnp.zeros((middle - skip, channels), jnp.float32), jnp.where(on_first, 0.0, tail)],
+            axis=0,
+        )
+        return own_low, first.astype(jnp.bfloat16), second.astype(jnp.bfloat16)
+
     def transform(number, held):
+        ready = prepare(number, 0)
         for g in range(group):
-            own_low = low[first_pair + number * group + g]
-            lower = degrees - 1 - own_low
-            coeffs = jnp.dot(spec[g], split[...], preferred_element_type=jnp.float32)
-            tail = coeffs[middle:]
-            on_first = lax.broadcasted_iota(jnp.int32, tail.shape, 0) < lower - middle
-            first = jnp.concatenate([coeffs[:middle], jnp.where(on_first, tail, 0.0)], axis=0)
-            second = jnp.concatenate(
-                [jnp.zeros((middle - skip, channels), jnp.float32), jnp.where(on_first, 0.0, tail)],
-                axis=0,
-            )
+            own_low, first, second = ready
+            if g + 1 < group:
+                ready = prepare(number, g + 1)
             sides = (
-                jnp.dot(leg[g], first.astype(jnp.bfloat16), preferred_element_type=jnp.float32),
-                jnp.dot(
-                    leg[g, :, skip:],
-                    second.astype(jnp.bfloat16),
-                    preferred_element_type=jnp.float32,
-                ),
+                jnp.dot(leg[g], first, preferred_element_type=jnp.float32),
+                jnp.dot(leg[g, :, skip:], second, preferred_element_type=jnp.float32),
             )
             for s in range(2):
                 parity = (own_low + s) % 2
@@ -272,21 +275,37 @@
 
 
 def network_kernel(cols, weight_in, weight_mid, weight_out, out):
-    rows = out.shape[0] // 2
-    for half in range(2):
-        own = slice(half * rows, (half + 1) * rows)
-        hidden = jnp.dot(cols[own], weight_in[...], preferred_element_type=jnp.float32)
-        hidden = silu(hidden).astype(jnp.bfloat16)
-        deeper = jnp.dot(hidden, weight_mid[...], preferred_element_type=jnp.float32)
-        deeper = silu(deeper).astype(jnp.bfloat16)
+    parts = 2
+    rows = out.shape[0] // parts
+
+    def enter(part):
+        hidden = jnp.dot(
+            cols[part * rows : (part + 1) * rows],
+            weight_in[...],
+            preferred_element_type=jnp.float32,
+        )
+        return silu(hidden).astype(jnp.bfloat16)
+
+    def leave(part, deeper):
         result = jnp.dot(deeper, weight_out[...], preferred_element_type=jnp.float32)
-        out[own] = result.astype(jnp.bfloat16)
+        out[part * rows : (part + 1) * rows] = result.astype(jnp.bfloat16)
+
+    hidden, deeper = enter(0), None
+    for part in range(parts):
+        current = hidden
+        if part + 1 < parts:
+            hidden = enter(part + 1)
+        middle = jnp.dot(current, weight_mid[...], preferred_element_type=jnp.float32)
+        if deeper is not None:
+            leave(part - 1, deeper)
+        deeper = silu(middle).astype(jnp.bfloat16)
+    leave(parts - 1, deeper)
 
 
 def network(columns, weight_in, weight_mid, weight_out):
     rows, feat = columns.shape
     hid = weight_in.shape[1]
-    block = rows // 8
+    block = rows // 4
     return pl.pallas_call(
         network_kernel,
         grid=(rows // block,),
@@ -425,6 +444,7 @@
     first_pair = lax.axis_index("wave") * steps * group
 
     def transform(number, held):
+        waiting = None
         for g in range(group):
             own_low = low[first_pair + number * group + g]
             lower = degrees - 1 - own_low
@@ -438,14 +458,20 @@
                 sides.append(jnp.concatenate(parts, axis=1).astype(jnp.bfloat16))
             first = jnp.dot(leg[g], sides[0], preferred_element_type=jnp.float32)
             second = jnp.dot(leg[g, middle:], sides[1], preferred_element_type=jnp.float32)
+            if waiting is not None:
+                finish(g - 1, waiting)
             on_first = lax.broadcasted_iota(jnp.int32, second.shape, 0) < lower - middle
             chosen = jnp.concatenate(
                 [first[:middle], jnp.where(on_first, first[middle:], second)], axis=0
             )
-            out[g] = jnp.dot(
-                chosen.astype(jnp.bfloat16), merge[...], preferred_element_type=jnp.float32
-            ).astype(jnp.bfloat16)
+            waiting = chosen.astype(jnp.bfloat16)
             yield
+        finish(group - 1, waiting)
+
+    def finish(g, chosen):
+        out[g] = jnp.dot(chosen, merge[...], preferred_element_type=jnp.float32).astype(
+            jnp.bfloat16
+        )
 
     staggered(step, steps, turn, transform, slots)
 

time: 464 us -> 460 us (level)
  no operation moved by 1% of the time
where the time goes in v5:
time: 460 us; the launch traced here: 459 us
  waiting for transfers between devices  240 us (52%)
  blocking collectives  85.2 us (19%)
  Pallas kernels  74.4 us (16%)
  other arithmetic  31.1 us (7%)
  local copies, waits for them, and re-layouts  15 us (3%)
  starting transfers between devices  13.4 us (3%)
    all_to_all x2, waiting for transfers between devices, exchange(): lax.all_to_all(blocks, 'wave', split_axis=0, concat_axis=0, tiled=True)  240 us
    all_to_all x2, blocking collectives, exchange(): lax.all_to_all(blocks, 'wave', split_axis=0, concat_axis=0, tiled=True)  85.2 us
    convert_element_type x1, other arithmetic, zonal_tables(): return (inverse.astype(jnp.bfloat16), forward.astype(jnp.bfloat16))  25.9 us
    pallas_call x1, Pallas kernels, network(): pl.pallas_call(network_kernel, grid=(rows // block,), in_specs=[pl.BlockS...  21.3 us
    unnamed x11, local copies, waits for them, and re-layouts  14 us
    pallas_call x1, Pallas kernels, forward_legendre(): pl.pallas_call(functools.partial(forward_legendre_kernel, steps), grid=(s...  13.5 us
    all_to_all x2, starting transfers between devices, exchange(): lax.all_to_all(blocks, 'wave', split_axis=0, concat_axis=0, tiled=True)  13.4 us
    pallas_call x1, Pallas kernels, inverse_legendre(): pl.pallas_call(functools.partial(inverse_legendre_kernel, steps), grid=(s...  13.3 us
  transfers between devices with their start and end apart: 2, of which 2 were waited for; matrix products, arithmetic and copies ran while one was open for 10% of the time, Pallas kernels for 0%

profile of v5, /device:TPU:13, one launch (start us, length us, event | category | flops | bytes accessed | tf_op | source)
XLA Modules:
  0.0 459.0 jit_solution(17630541996829788822)
XLA Ops:
  0.0 13.3 %inverse_legendre.1 = bf16[16,40,5120]{2,1,0:T(8,128)(2,1)} custom-call(s32[320]{0:T(512)} %low.3, bf16[20,641,256]{2,1,0:T(8,128)(2,1)} %spec.1, bf16[20,320,641]{2,1,0:T(8,128)(2,1)} %bitcast.32, bf16[256,256]{1,0:T(8,128)(2,1)} %constant.77.clone.split), custom_call_target="tpu_custom_call" | custom-call | tf_op jit(solution)/shard_map/inverse_legendre/pallas_call | solution.py:163
  13.3 6.7 %all-to-all-start = ((bf16[16,40,5120]{2,1,0:T(8,128)(2,1)}), bf16[16,40,5120]{2,1,0:T(8,128)(2,1)}, u32[]{:S(2)}, u32[]{:S(2)}) async-start(bf16[16,40,5120]{2,1,0:T(8,128)(2,1)} %inverse_legendre.1), calls=%async_computation | async-start | bytes 13107200 | tf_op jit(solution)/shard_map/all_to_all | solution.py:505
  19.9 0.0 copy-done.3
  20.0 0.1 broadcast_in_dim.26
  20.2 0.0 copy-done.4
  20.2 4.6 %reduce-window.6 = s32[16,25,128]{2,1,0:T(8,128)S(1)} reduce-window(s32[16,25,128]{2,1,0:T(8,128)S(1)} %fusion.16, s32[]{:T(128)} %constant.65.clone.1), window={size=1x1x128 pad=0_0x0_0x127_0}, to_apply=%region_0.1 | reduce-window | flops 6502400 | bytes 409604 | tf_op jit(solution)/shard_map/reduce-window
  24.9 0.5 slice_reduce_fusion
  25.3 0.2 reduce-window.9
  25.5 0.1 broadcast_in_dim.24
  25.7 0.2 mul.76
  25.9 0.1 add_add_fusion
  26.1 0.1 fusion.18
  26.2 25.9 %fusion.9 = (bf16[2,640,640]{2,1,0:T(8,128)(2,1)S(1)}, bf16[2,640,640]{2,1,0:T(8,128)(2,1)S(1)}) fusion(s32[640]{0:T(1024)S(1)} %broadcast_in_dim.26, s32[640]{0:T(1024)S(1)} %fusion.25, s32[2,640]{1,0:T(2,128)S(1)} %mul.76, f32[2,640]{1,0:T(2,128)S(1)} %compare_select_fusion), kind=kLoop, calls=%fused_computation.11 | loop fusion | flops 19660800 | bytes 3292160 | tf_op jit(solution)/shard_map/convert_element_type | solution.py:55
  52.1 110.8 %all-to-all-done = bf16[16,40,5120]{2,1,0:T(8,128)(2,1)} async-done(((bf16[16,40,5120]{2,1,0:T(8,128)(2,1)}), bf16[16,40,5120]{2,1,0:T(8,128)(2,1)}, u32[]{:S(2)}, u32[]{:S(2)}) %all-to-all-start) | async-done | bytes 6553632 | tf_op jit(solution)/shard_map/all_to_all | solution.py:505
  163.0 13.1 %to_grid.1 = (bf16[1280,2560]{1,0:T(8,128)(2,1)}, bf16[6400,128]{1,0:T(8,128)(2,1)S(1)}) custom-call(s32[3200]{0:T(1024)S(1)} %multiply_add_fusion.slots, bf16[2,640,640]{2,1,0:T(8,128)(2,1)S(1)} %get-tuple-element.11.table, bf16[640,5120]{1,0:T(8,128)(2,1)} %bitcast.2.coeffs), custom_call_target="tpu_custom_call" | custom-call | tf_op jit(solution)/shard_map/to_grid/pallas_call | solution.py:244
  176.1 42.6 %all_to_all.20 = bf16[16,400,128]{2,1,0:T(8,128)(2,1)S(1)} all-to-all(bf16[16,400,128]{2,1,0:T(8,128)(2,1)S(1)} %bitcast.29), channel_id=1, replica_groups=mesh['grp'=2,'wave'=16] {'wave'}, dimensions={0} | all-to-all | bytes 3276800 | tf_op jit(solution)/shard_map/all_to_all | solution.py:505
  218.6 0.0 copy-done
  218.6 21.3 %network.1 = bf16[6400,128]{1,0:T(8,128)(2,1)S(1)} custom-call(bf16[6400,128]{1,0:T(8,128)(2,1)S(1)} %bitcast.26, bf16[128,1024]{1,0:T(8,128)(2,1)S(1)} %bitcast.30, bf16[1024,1024]{1,0:T(8,128)(2,1)S(1)} %bitcast.28, bf16[1024,128]{1,0:T(8,128)(2,1)S(1)} %bitcast.31), custom_call_target="tpu_custom_call" | custom-call | tf_op jit(solution)/shard_map/network/pallas_call | solution.py:309
  240.0 42.6 %all_to_all.21 = bf16[16,400,128]{2,1,0:T(8,128)(2,1)S(1)} all-to-all(bf16[16,400,128]{2,1,0:T(8,128)(2,1)S(1)} %bitcast.27), channel_id=1, replica_groups=mesh['grp'=2,'wave'=16] {'wave'}, dimensions={0} | all-to-all | bytes 3276800 | tf_op jit(solution)/shard_map/all_to_all | solution.py:505
  282.6 13.2 %to_waves.1 = bf16[640,5120]{1,0:T(8,128)(2,1)} custom-call(s32[3200]{0:T(1024)S(1)} %multiply_add_fusion.slots, bf16[2,640,640]{2,1,0:T(8,128)(2,1)S(1)} %get-tuple-element.12.table, bf16[1280,2560]{1,0:T(8,128)(2,1)} %get-tuple-element.7.forced, bf16[6400,128]{1,0:T(8,128)(2,1)S(1)} %bitcast.25), custom_call_target="tpu_custom_call" | custom-call | tf_op jit(solution)/shard_map/to_waves/pallas_call | solution.py:399
  295.8 6.7 %all-to-all-start.3 = ((bf16[16,40,5120]{2,1,0:T(8,128)(2,1)}), bf16[16,40,5120]{2,1,0:T(8,128)(2,1)}, u32[]{:S(2)}, u32[]{:S(2)}) async-start(bf16[16,40,5120]{2,1,0:T(8,128)(2,1)} %bitcast.33), calls=%async_computation.3 | async-start | bytes 13107200 | tf_op jit(solution)/shard_map/all_to_all | solution.py:505
  302.5 14.0 %copy.12.leg = bf16[20,641,320]{2,1,0:T(8,128)(2,1)} copy(bf16[20,641,320]{1,2,0:T(8,128)(2,1)} %param.11) | data formatting | bytes 16409600 | tf_op args[1]
  316.5 129.0 %all-to-all-done.3.coeffs = bf16[16,40,5120]{2,1,0:T(8,128)(2,1)} async-done(((bf16[16,40,5120]{2,1,0:T(8,128)(2,1)}), bf16[16,40,5120]{2,1,0:T(8,128)(2,1)}, u32[]{:S(2)}, u32[]{:S(2)}) %all-to-all-start.3) | async-done | bytes 6553632 | tf_op jit(solution)/shard_map/all_to_all | solution.py:505
  445.5 13.5 %forward_legendre.1 = bf16[20,641,256]{2,1,0:T(8,128)(2,1)} custom-call(s32[320]{0:T(512)} %low.3, bf16[16,40,5120]{2,1,0:T(8,128)(2,1)} %all-to-all-done.3.coeffs, bf16[20,641,320]{2,1,0:T(8,128)(2,1)} %copy.12.leg, bf16[256,256]{1,0:T(8,128)(2,1)} %constant.79.clone.merge), custom_call_target="tpu_custom_call" | custom-call | tf_op jit(solution)/shard_map/forward_legendre/pallas_call | solution.py:485
  (18 shorter events, 0.1 us)
Async XLA Ops:
  13.3 6.7 %copy-start.3 = (s32[320]{0:T(512)S(1)}, s32[320]{0:T(512)}, u32[]{:S(2)}) copy-start(s32[320]{0:T(512)} %low.3) | copy-start | bytes 3844
  13.3 6.9 %copy-start.4 = (s32[3200,1]{0,1:T(1,128)S(1)}, s32[3200,1]{0,1:T(1,128)}, u32[]{:S(2)}) copy-start(s32[3200,1]{0,1:T(1,128)} %param.13) | copy-start | bytes 38404
  13.3 149.7 %all-to-all-start = ((bf16[16,40,5120]{2,1,0:T(8,128)(2,1)}), bf16[16,40,5120]{2,1,0:T(8,128)(2,1)}, u32[]{:S(2)}, u32[]{:S(2)}) async-start(bf16[16,40,5120]{2,1,0:T(8,128)(2,1)} %inverse_legendre.1), calls=%async_computation | async-start | bytes 13107200 | tf_op jit(solution)/shard_map/all_to_all | solution.py:505
  176.1 42.6 %copy-start = (bf16[1,1024,1024]{2,1,0:T(8,128)(2,1)S(1)}, bf16[1,1024,1024]{2,1,0:T(8,128)(2,1)}, u32[]{:S(2)}) copy-start(bf16[1,1024,1024]{2,1,0:T(8,128)(2,1)} %param.15) | copy-start | bytes 6291460
  176.1 42.6 %copy-start.1 = (bf16[1,128,1024]{2,1,0:T(8,128)(2,1)S(1)}, bf16[1,128,1024]{2,1,0:T(8,128)(2,1)}, u32[]{:S(2)}) copy-start(bf16[1,128,1024]{2,1,0:T(8,128)(2,1)} %param.14) | copy-start | bytes 786436
  176.1 42.6 %copy-start.2 = (bf16[1,1024,128]{2,1,0:T(8,128)(2,1)S(1)}, bf16[1,1024,128]{2,1,0:T(8,128)(2,1)}, u32[]{:S(2)}) copy-start(bf16[1,1024,128]{2,1,0:T(8,128)(2,1)} %param.16) | copy-start | bytes 786436
  295.8 149.7 %all-to-all-start.3 = ((bf16[16,40,5120]{2,1,0:T(8,128)(2,1)}), bf16[16,40,5120]{2,1,0:T(8,128)(2,1)}, u32[]{:S(2)}, u32[]{:S(2)}) async-start(bf16[16,40,5120]{2,1,0:T(8,128)(2,1)} %bitcast.33), calls=%async_computation.3 | async-start | bytes 13107200 | tf_op jit(solution)/shard_map/all_to_all | solution.py:505

commit v6 on v5

--- a/solution.py
+++ b/solution.py
@@ -159,7 +159,7 @@
     lanes = lat_total // devices * channels
     group = group_of(pairs)
     steps = pairs // group
-    slot = pltpu.VMEM((4 * group * (lat_total + PITCH_EXTRA), channels // 2), jnp.float32)
+    slot = pltpu.VMEM(((4 * group + 1) * (lat_total + PITCH_EXTRA), channels // 2), jnp.float32)
     return pl.pallas_call(
         functools.partial(inverse_legendre_kernel, steps),
         grid=(steps + 1,),
@@ -481,7 +481,7 @@
     pairs, degrees, lat_total = legendre.shape
     group = group_of(pairs)
     steps = pairs // group
-    slot = pltpu.VMEM((4 * group * (lat_total + PITCH_EXTRA), channels // 2), jnp.float32)
+    slot = pltpu.VMEM(((4 * group + 1) * (lat_total + PITCH_EXTRA), channels // 2), jnp.float32)
     return pl.pallas_call(
         functools.partial(forward_legendre_kernel, steps),
         grid=(steps + 1,),

time: 460 us -> 460 us (level)
  no operation moved by 1% of the time
where the time goes in v6:
time: 460 us; the launch traced here: 459 us
  waiting for transfers between devices  240 us (52%)
  blocking collectives  85.2 us (19%)
  Pallas kernels  74.4 us (16%)
  other arithmetic  31.1 us (7%)
  local copies, waits for them, and re-layouts  15 us (3%)
  starting transfers between devices  13.3 us (3%)
    all_to_all x2, waiting for transfers between devices, exchange(): lax.all_to_all(blocks, 'wave', split_axis=0, concat_axis=0, tiled=True)  240 us
    all_to_all x2, blocking collectives, exchange(): lax.all_to_all(blocks, 'wave', split_axis=0, concat_axis=0, tiled=True)  85.2 us
    convert_element_type x1, other arithmetic, zonal_tables(): return (inverse.astype(jnp.bfloat16), forward.astype(jnp.bfloat16))  25.9 us
    pallas_call x1, Pallas kernels, network(): pl.pallas_call(network_kernel, grid=(rows // block,), in_specs=[pl.BlockS...  21.3 us
    unnamed x11, local copies, waits for them, and re-layouts  14 us
    pallas_call x1, Pallas kernels, forward_legendre(): pl.pallas_call(functools.partial(forward_legendre_kernel, steps), grid=(s...  13.5 us
    all_to_all x2, starting transfers between devices, exchange(): lax.all_to_all(blocks, 'wave', split_axis=0, concat_axis=0, tiled=True)  13.3 us
    pallas_call x1, Pallas kernels, inverse_legendre(): pl.pallas_call(functools.partial(inverse_legendre_kernel, steps), grid=(s...  13.3 us
  transfers between devices with their start and end apart: 2, of which 2 were waited for; matrix products, arithmetic and copies ran while one was open for 10% of the time, Pallas kernels for 0%

profile of v6, /device:TPU:13, one launch (start us, length us, event | category | flops | bytes accessed | tf_op | source)
XLA Modules:
  0.0 459.0 jit_solution(10632122792533308426)
XLA Ops:
  0.0 13.3 %inverse_legendre.1 = bf16[16,40,5120]{2,1,0:T(8,128)(2,1)} custom-call(s32[320]{0:T(512)} %low.3, bf16[20,641,256]{2,1,0:T(8,128)(2,1)} %spec.1, bf16[20,320,641]{2,1,0:T(8,128)(2,1)} %bitcast.32, bf16[256,256]{1,0:T(8,128)(2,1)} %constant.77.clone.split), custom_call_target="tpu_custom_call" | custom-call | tf_op jit(solution)/shard_map/inverse_legendre/pallas_call | solution.py:163
  13.3 6.7 %all-to-all-start = ((bf16[16,40,5120]{2,1,0:T(8,128)(2,1)}), bf16[16,40,5120]{2,1,0:T(8,128)(2,1)}, u32[]{:S(2)}, u32[]{:S(2)}) async-start(bf16[16,40,5120]{2,1,0:T(8,128)(2,1)} %inverse_legendre.1), calls=%async_computation | async-start | bytes 13107200 | tf_op jit(solution)/shard_map/all_to_all | solution.py:505
  19.9 0.0 copy-done.3
  20.0 0.1 broadcast_in_dim.26
  20.2 0.0 copy-done.4
  20.2 4.6 %reduce-window.6 = s32[16,25,128]{2,1,0:T(8,128)S(1)} reduce-window(s32[16,25,128]{2,1,0:T(8,128)S(1)} %fusion.16, s32[]{:T(128)} %constant.65.clone.1), window={size=1x1x128 pad=0_0x0_0x127_0}, to_apply=%region_0.1 | reduce-window | flops 6502400 | bytes 409604 | tf_op jit(solution)/shard_map/reduce-window
  24.9 0.5 slice_reduce_fusion
  25.3 0.2 reduce-window.9
  25.5 0.1 broadcast_in_dim.24
  25.7 0.2 mul.76
  25.9 0.1 add_add_fusion
  26.1 0.1 fusion.18
  26.2 25.9 %fusion.9 = (bf16[2,640,640]{2,1,0:T(8,128)(2,1)S(1)}, bf16[2,640,640]{2,1,0:T(8,128)(2,1)S(1)}) fusion(s32[640]{0:T(1024)S(1)} %broadcast_in_dim.26, s32[640]{0:T(1024)S(1)} %fusion.25, s32[2,640]{1,0:T(2,128)S(1)} %mul.76, f32[2,640]{1,0:T(2,128)S(1)} %compare_select_fusion), kind=kLoop, calls=%fused_computation.11 | loop fusion | flops 19660800 | bytes 3292160 | tf_op jit(solution)/shard_map/convert_element_type | solution.py:55
  52.1 110.8 %all-to-all-done = bf16[16,40,5120]{2,1,0:T(8,128)(2,1)} async-done(((bf16[16,40,5120]{2,1,0:T(8,128)(2,1)}), bf16[16,40,5120]{2,1,0:T(8,128)(2,1)}, u32[]{:S(2)}, u32[]{:S(2)}) %all-to-all-start) | async-done | bytes 6553632 | tf_op jit(solution)/shard_map/all_to_all | solution.py:505
  163.0 13.1 %to_grid.1 = (bf16[1280,2560]{1,0:T(8,128)(2,1)}, bf16[6400,128]{1,0:T(8,128)(2,1)S(1)}) custom-call(s32[3200]{0:T(1024)S(1)} %multiply_add_fusion.slots, bf16[2,640,640]{2,1,0:T(8,128)(2,1)S(1)} %get-tuple-element.11.table, bf16[640,5120]{1,0:T(8,128)(2,1)} %bitcast.2.coeffs), custom_call_target="tpu_custom_call" | custom-call | tf_op jit(solution)/shard_map/to_grid/pallas_call | solution.py:244
  176.1 42.6 %all_to_all.20 = bf16[16,400,128]{2,1,0:T(8,128)(2,1)S(1)} all-to-all(bf16[16,400,128]{2,1,0:T(8,128)(2,1)S(1)} %bitcast.29), channel_id=1, replica_groups=mesh['grp'=2,'wave'=16] {'wave'}, dimensions={0} | all-to-all | bytes 3276800 | tf_op jit(solution)/shard_map/all_to_all | solution.py:505
  218.6 0.0 copy-done
  218.6 21.3 %network.1 = bf16[6400,128]{1,0:T(8,128)(2,1)S(1)} custom-call(bf16[6400,128]{1,0:T(8,128)(2,1)S(1)} %bitcast.26, bf16[128,1024]{1,0:T(8,128)(2,1)S(1)} %bitcast.30, bf16[1024,1024]{1,0:T(8,128)(2,1)S(1)} %bitcast.28, bf16[1024,128]{1,0:T(8,128)(2,1)S(1)} %bitcast.31), custom_call_target="tpu_custom_call" | custom-call | tf_op jit(solution)/shard_map/network/pallas_call | solution.py:309
  240.0 42.6 %all_to_all.21 = bf16[16,400,128]{2,1,0:T(8,128)(2,1)S(1)} all-to-all(bf16[16,400,128]{2,1,0:T(8,128)(2,1)S(1)} %bitcast.27), channel_id=1, replica_groups=mesh['grp'=2,'wave'=16] {'wave'}, dimensions={0} | all-to-all | bytes 3276800 | tf_op jit(solution)/shard_map/all_to_all | solution.py:505
  282.6 13.2 %to_waves.1 = bf16[640,5120]{1,0:T(8,128)(2,1)} custom-call(s32[3200]{0:T(1024)S(1)} %multiply_add_fusion.slots, bf16[2,640,640]{2,1,0:T(8,128)(2,1)S(1)} %get-tuple-element.12.table, bf16[1280,2560]{1,0:T(8,128)(2,1)} %get-tuple-element.7.forced, bf16[6400,128]{1,0:T(8,128)(2,1)S(1)} %bitcast.25), custom_call_target="tpu_custom_call" | custom-call | tf_op jit(solution)/shard_map/to_waves/pallas_call | solution.py:399
  295.8 6.7 %all-to-all-start.3 = ((bf16[16,40,5120]{2,1,0:T(8,128)(2,1)}), bf16[16,40,5120]{2,1,0:T(8,128)(2,1)}, u32[]{:S(2)}, u32[]{:S(2)}) async-start(bf16[16,40,5120]{2,1,0:T(8,128)(2,1)} %bitcast.33), calls=%async_computation.3 | async-start | bytes 13107200 | tf_op jit(solution)/shard_map/all_to_all | solution.py:505
  302.5 14.0 %copy.12.leg = bf16[20,641,320]{2,1,0:T(8,128)(2,1)} copy(bf16[20,641,320]{1,2,0:T(8,128)(2,1)} %param.11) | data formatting | bytes 16409600 | tf_op args[1]
  316.5 129.0 %all-to-all-done.3.coeffs = bf16[16,40,5120]{2,1,0:T(8,128)(2,1)} async-done(((bf16[16,40,5120]{2,1,0:T(8,128)(2,1)}), bf16[16,40,5120]{2,1,0:T(8,128)(2,1)}, u32[]{:S(2)}, u32[]{:S(2)}) %all-to-all-start.3) | async-done | bytes 6553632 | tf_op jit(solution)/shard_map/all_to_all | solution.py:505
  445.5 13.5 %forward_legendre.1 = bf16[20,641,256]{2,1,0:T(8,128)(2,1)} custom-call(s32[320]{0:T(512)} %low.3, bf16[16,40,5120]{2,1,0:T(8,128)(2,1)} %all-to-all-done.3.coeffs, bf16[20,641,320]{2,1,0:T(8,128)(2,1)} %copy.12.leg, bf16[256,256]{1,0:T(8,128)(2,1)} %constant.79.clone.merge), custom_call_target="tpu_custom_call" | custom-call | tf_op jit(solution)/shard_map/forward_legendre/pallas_call | solution.py:485
  (18 shorter events, 0.1 us)
Async XLA Ops:
  13.3 6.7 %copy-start.3 = (s32[320]{0:T(512)S(1)}, s32[320]{0:T(512)}, u32[]{:S(2)}) copy-start(s32[320]{0:T(512)} %low.3) | copy-start | bytes 3844
  13.3 6.9 %copy-start.4 = (s32[3200,1]{0,1:T(1,128)S(1)}, s32[3200,1]{0,1:T(1,128)}, u32[]{:S(2)}) copy-start(s32[3200,1]{0,1:T(1,128)} %param.13) | copy-start | bytes 38404
  13.3 149.7 %all-to-all-start = ((bf16[16,40,5120]{2,1,0:T(8,128)(2,1)}), bf16[16,40,5120]{2,1,0:T(8,128)(2,1)}, u32[]{:S(2)}, u32[]{:S(2)}) async-start(bf16[16,40,5120]{2,1,0:T(8,128)(2,1)} %inverse_legendre.1), calls=%async_computation | async-start | bytes 13107200 | tf_op jit(solution)/shard_map/all_to_all | solution.py:505
  176.1 42.6 %copy-start = (bf16[1,1024,1024]{2,1,0:T(8,128)(2,1)S(1)}, bf16[1,1024,1024]{2,1,0:T(8,128)(2,1)}, u32[]{:S(2)}) copy-start(bf16[1,1024,1024]{2,1,0:T(8,128)(2,1)} %param.15) | copy-start | bytes 6291460
  176.1 42.6 %copy-start.1 = (bf16[1,128,1024]{2,1,0:T(8,128)(2,1)S(1)}, bf16[1,128,1024]{2,1,0:T(8,128)(2,1)}, u32[]{:S(2)}) copy-start(bf16[1,128,1024]{2,1,0:T(8,128)(2,1)} %param.14) | copy-start | bytes 786436
  176.1 42.6 %copy-start.2 = (bf16[1,1024,128]{2,1,0:T(8,128)(2,1)S(1)}, bf16[1,1024,128]{2,1,0:T(8,128)(2,1)}, u32[]{:S(2)}) copy-start(bf16[1,1024,128]{2,1,0:T(8,128)(2,1)} %param.16) | copy-start | bytes 786436
  295.8 149.7 %all-to-all-start.3 = ((bf16[16,40,5120]{2,1,0:T(8,128)(2,1)}), bf16[16,40,5120]{2,1,0:T(8,128)(2,1)}, u32[]{:S(2)}, u32[]{:S(2)}) async-start(bf16[16,40,5120]{2,1,0:T(8,128)(2,1)} %bitcast.33), calls=%async_computation.3 | async-start | bytes 13107200 | tf_op jit(solution)/shard_map/all_to_all | solution.py:505

commit v7 on v6

--- a/solution.py
+++ b/solution.py
@@ -18,6 +18,9 @@
 
 def params(mebibytes):
     return pltpu.CompilerParams(vmem_limit_bytes=mebibytes * 1024 * 1024)
+
+
+WHOLE = pl.BlockSpec(memory_space=pltpu.VMEM)
 
 
 def in_hbm(array):
@@ -247,7 +250,7 @@
             num_scalar_prefetch=1,
             grid=(steps + 1,),
             in_specs=[
-                pl.BlockSpec((2, NLON // 2, depth), lambda i, s: (0, 0, 0)),
+                WHOLE,
                 pl.BlockSpec((depth, 2 * own), lambda i, s: (0, jnp.minimum(i, steps - 1))),
             ],
             out_specs=[
@@ -311,9 +314,9 @@
         grid=(rows // block,),
         in_specs=[
             pl.BlockSpec((block, feat), lambda i: (i, 0)),
-            pl.BlockSpec((feat, hid), lambda i: (0, 0)),
-            pl.BlockSpec((hid, hid), lambda i: (0, 0)),
-            pl.BlockSpec((hid, feat), lambda i: (0, 0)),
+            WHOLE,
+            WHOLE,
+            WHOLE,
         ],
         out_specs=pl.BlockSpec((block, feat), lambda i: (i, 0)),
         out_shape=jax.ShapeDtypeStruct((rows, feat), jnp.bfloat16),
@@ -402,9 +405,9 @@
             num_scalar_prefetch=1,
             grid=(steps + 1,),
             in_specs=[
-                pl.BlockSpec((2, depth, NLON // 2), lambda i, s: (0, 0, 0)),
+                WHOLE,
                 pl.BlockSpec((NLON, own), lambda i, s: (0, jnp.minimum(i, steps - 1))),
-                pl.BlockSpec((slot_total, feat), lambda i, s: (0, 0)),
+                WHOLE,
             ],
             out_specs=pl.BlockSpec((depth, 2 * own), lambda i, s: (0, jnp.maximum(i - 1, 0))),
             scratch_shapes=[

time: 460 us -> 460 us (level)
  no operation moved by 1% of the time
where the time goes in v7:
time: 460 us; the launch traced here: 459 us
  waiting for transfers between devices  240 us (52%)
  blocking collectives  85.2 us (19%)
  Pallas kernels  74.4 us (16%)
  other arithmetic  31.1 us (7%)
  local copies, waits for them, and re-layouts  15 us (3%)
  starting transfers between devices  13.3 us (3%)
    all_to_all x2, waiting for transfers between devices, exchange(): lax.all_to_all(blocks, 'wave', split_axis=0, concat_axis=0, tiled=True)  240 us
    all_to_all x2, blocking collectives, exchange(): lax.all_to_all(blocks, 'wave', split_axis=0, concat_axis=0, tiled=True)  85.2 us
    convert_element_type x1, other arithmetic, zonal_tables(): return (inverse.astype(jnp.bfloat16), forward.astype(jnp.bfloat16))  25.9 us
    pallas_call x1, Pallas kernels, network(): pl.pallas_call(network_kernel, grid=(rows // block,), in_specs=[pl.BlockS...  21.3 us
    unnamed x11, local copies, waits for them, and re-layouts  14 us
    pallas_call x1, Pallas kernels, forward_legendre(): pl.pallas_call(functools.partial(forward_legendre_kernel, steps), grid=(s...  13.5 us
    all_to_all x2, starting transfers between devices, exchange(): lax.all_to_all(blocks, 'wave', split_axis=0, concat_axis=0, tiled=True)  13.3 us
    pallas_call x1, Pallas kernels, inverse_legendre(): pl.pallas_call(functools.partial(inverse_legendre_kernel, steps), grid=(s...  13.3 us
  transfers between devices with their start and end apart: 2, of which 2 were waited for; matrix products, arithmetic and copies ran while one was open for 10% of the time, Pallas kernels for 0%

profile of v7, /device:TPU:13, one launch (start us, length us, event | category | flops | bytes accessed | tf_op | source)
XLA Modules:
  0.0 459.0 jit_solution(10632122792533308426)
XLA Ops:
  0.0 13.3 %inverse_legendre.1 = bf16[16,40,5120]{2,1,0:T(8,128)(2,1)} custom-call(s32[320]{0:T(512)} %low.3, bf16[20,641,256]{2,1,0:T(8,128)(2,1)} %spec.1, bf16[20,320,641]{2,1,0:T(8,128)(2,1)} %bitcast.32, bf16[256,256]{1,0:T(8,128)(2,1)} %constant.77.clone.split), custom_call_target="tpu_custom_call" | custom-call | tf_op jit(solution)/shard_map/inverse_legendre/pallas_call | solution.py:166
  13.3 6.7 %all-to-all-start = ((bf16[16,40,5120]{2,1,0:T(8,128)(2,1)}), bf16[16,40,5120]{2,1,0:T(8,128)(2,1)}, u32[]{:S(2)}, u32[]{:S(2)}) async-start(bf16[16,40,5120]{2,1,0:T(8,128)(2,1)} %inverse_legendre.1), calls=%async_computation | async-start | bytes 13107200 | tf_op jit(solution)/shard_map/all_to_all | solution.py:508
  19.9 0.0 copy-done.3
  20.0 0.1 broadcast_in_dim.26
  20.2 0.0 copy-done.4
  20.2 4.6 %reduce-window.6 = s32[16,25,128]{2,1,0:T(8,128)S(1)} reduce-window(s32[16,25,128]{2,1,0:T(8,128)S(1)} %fusion.16, s32[]{:T(128)} %constant.65.clone.1), window={size=1x1x128 pad=0_0x0_0x127_0}, to_apply=%region_0.1 | reduce-window | flops 6502400 | bytes 409604 | tf_op jit(solution)/shard_map/reduce-window
  24.9 0.5 slice_reduce_fusion
  25.3 0.2 reduce-window.9
  25.5 0.1 broadcast_in_dim.24
  25.7 0.2 mul.76
  25.9 0.1 add_add_fusion
  26.1 0.1 fusion.18
  26.2 25.9 %fusion.9 = (bf16[2,640,640]{2,1,0:T(8,128)(2,1)S(1)}, bf16[2,640,640]{2,1,0:T(8,128)(2,1)S(1)}) fusion(s32[640]{0:T(1024)S(1)} %broadcast_in_dim.26, s32[640]{0:T(1024)S(1)} %fusion.25, s32[2,640]{1,0:T(2,128)S(1)} %mul.76, f32[2,640]{1,0:T(2,128)S(1)} %compare_select_fusion), kind=kLoop, calls=%fused_computation.11 | loop fusion | flops 19660800 | bytes 3292160 | tf_op jit(solution)/shard_map/convert_element_type | solution.py:58
  52.1 110.8 %all-to-all-done = bf16[16,40,5120]{2,1,0:T(8,128)(2,1)} async-done(((bf16[16,40,5120]{2,1,0:T(8,128)(2,1)}), bf16[16,40,5120]{2,1,0:T(8,128)(2,1)}, u32[]{:S(2)}, u32[]{:S(2)}) %all-to-all-start) | async-done | bytes 6553632 | tf_op jit(solution)/shard_map/all_to_all | solution.py:508
  163.0 13.1 %to_grid.1 = (bf16[1280,2560]{1,0:T(8,128)(2,1)}, bf16[6400,128]{1,0:T(8,128)(2,1)S(1)}) custom-call(s32[3200]{0:T(1024)S(1)} %multiply_add_fusion.slots, bf16[2,640,640]{2,1,0:T(8,128)(2,1)S(1)} %get-tuple-element.11.table, bf16[640,5120]{1,0:T(8,128)(2,1)} %bitcast.2.coeffs), custom_call_target="tpu_custom_call" | custom-call | tf_op jit(solution)/shard_map/to_grid/pallas_call | solution.py:247
  176.1 42.6 %all_to_all.20 = bf16[16,400,128]{2,1,0:T(8,128)(2,1)S(1)} all-to-all(bf16[16,400,128]{2,1,0:T(8,128)(2,1)S(1)} %bitcast.29), channel_id=1, replica_groups=mesh['grp'=2,'wave'=16] {'wave'}, dimensions={0} | all-to-all | bytes 3276800 | tf_op jit(solution)/shard_map/all_to_all | solution.py:508
  218.6 0.0 copy-done
  218.6 21.3 %network.1 = bf16[6400,128]{1,0:T(8,128)(2,1)S(1)} custom-call(bf16[6400,128]{1,0:T(8,128)(2,1)S(1)} %bitcast.26, bf16[128,1024]{1,0:T(8,128)(2,1)S(1)} %bitcast.30, bf16[1024,1024]{1,0:T(8,128)(2,1)S(1)} %bitcast.28, bf16[1024,128]{1,0:T(8,128)(2,1)S(1)} %bitcast.31), custom_call_target="tpu_custom_call" | custom-call | tf_op jit(solution)/shard_map/network/pallas_call | solution.py:312
  240.0 42.6 %all_to_all.21 = bf16[16,400,128]{2,1,0:T(8,128)(2,1)S(1)} all-to-all(bf16[16,400,128]{2,1,0:T(8,128)(2,1)S(1)} %bitcast.27), channel_id=1, replica_groups=mesh['grp'=2,'wave'=16] {'wave'}, dimensions={0} | all-to-all | bytes 3276800 | tf_op jit(solution)/shard_map/all_to_all | solution.py:508
  282.6 13.2 %to_waves.1 = bf16[640,5120]{1,0:T(8,128)(2,1)} custom-call(s32[3200]{0:T(1024)S(1)} %multiply_add_fusion.slots, bf16[2,640,640]{2,1,0:T(8,128)(2,1)S(1)} %get-tuple-element.12.table, bf16[1280,2560]{1,0:T(8,128)(2,1)} %get-tuple-element.7.forced, bf16[6400,128]{1,0:T(8,128)(2,1)S(1)} %bitcast.25), custom_call_target="tpu_custom_call" | custom-call | tf_op jit(solution)/shard_map/to_waves/pallas_call | solution.py:402
  295.9 6.6 %all-to-all-start.3 = ((bf16[16,40,5120]{2,1,0:T(8,128)(2,1)}), bf16[16,40,5120]{2,1,0:T(8,128)(2,1)}, u32[]{:S(2)}, u32[]{:S(2)}) async-start(bf16[16,40,5120]{2,1,0:T(8,128)(2,1)} %bitcast.33), calls=%async_computation.3 | async-start | bytes 13107200 | tf_op jit(solution)/shard_map/all_to_all | solution.py:508
  302.5 14.0 %copy.12.leg = bf16[20,641,320]{2,1,0:T(8,128)(2,1)} copy(bf16[20,641,320]{1,2,0:T(8,128)(2,1)} %param.11) | data formatting | bytes 16409600 | tf_op args[1]
  316.5 129.0 %all-to-all-done.3.coeffs = bf16[16,40,5120]{2,1,0:T(8,128)(2,1)} async-done(((bf16[16,40,5120]{2,1,0:T(8,128)(2,1)}), bf16[16,40,5120]{2,1,0:T(8,128)(2,1)}, u32[]{:S(2)}, u32[]{:S(2)}) %all-to-all-start.3) | async-done | bytes 6553632 | tf_op jit(solution)/shard_map/all_to_all | solution.py:508
  445.5 13.5 %forward_legendre.1 = bf16[20,641,256]{2,1,0:T(8,128)(2,1)} custom-call(s32[320]{0:T(512)} %low.3, bf16[16,40,5120]{2,1,0:T(8,128)(2,1)} %all-to-all-done.3.coeffs, bf16[20,641,320]{2,1,0:T(8,128)(2,1)} %copy.12.leg, bf16[256,256]{1,0:T(8,128)(2,1)} %constant.79.clone.merge), custom_call_target="tpu_custom_call" | custom-call | tf_op jit(solution)/shard_map/forward_legendre/pallas_call | solution.py:488
  (18 shorter events, 0.1 us)
Async XLA Ops:
  13.3 6.7 %copy-start.3 = (s32[320]{0:T(512)S(1)}, s32[320]{0:T(512)}, u32[]{:S(2)}) copy-start(s32[320]{0:T(512)} %low.3) | copy-start | bytes 3844
  13.3 6.9 %copy-start.4 = (s32[3200,1]{0,1:T(1,128)S(1)}, s32[3200,1]{0,1:T(1,128)}, u32[]{:S(2)}) copy-start(s32[3200,1]{0,1:T(1,128)} %param.13) | copy-start | bytes 38404
  13.3 149.7 %all-to-all-start = ((bf16[16,40,5120]{2,1,0:T(8,128)(2,1)}), bf16[16,40,5120]{2,1,0:T(8,128)(2,1)}, u32[]{:S(2)}, u32[]{:S(2)}) async-start(bf16[16,40,5120]{2,1,0:T(8,128)(2,1)} %inverse_legendre.1), calls=%async_computation | async-start | bytes 13107200 | tf_op jit(solution)/shard_map/all_to_all | solution.py:508
  176.1 42.6 %copy-start = (bf16[1,1024,1024]{2,1,0:T(8,128)(2,1)S(1)}, bf16[1,1024,1024]{2,1,0:T(8,128)(2,1)}, u32[]{:S(2)}) copy-start(bf16[1,1024,1024]{2,1,0:T(8,128)(2,1)} %param.15) | copy-start | bytes 6291460
  176.1 42.6 %copy-start.1 = (bf16[1,128,1024]{2,1,0:T(8,128)(2,1)S(1)}, bf16[1,128,1024]{2,1,0:T(8,128)(2,1)}, u32[]{:S(2)}) copy-start(bf16[1,128,1024]{2,1,0:T(8,128)(2,1)} %param.14) | copy-start | bytes 786436
  176.1 42.6 %copy-start.2 = (bf16[1,1024,128]{2,1,0:T(8,128)(2,1)S(1)}, bf16[1,1024,128]{2,1,0:T(8,128)(2,1)}, u32[]{:S(2)}) copy-start(bf16[1,1024,128]{2,1,0:T(8,128)(2,1)} %param.16) | copy-start | bytes 786436
  295.9 149.7 %all-to-all-start.3 = ((bf16[16,40,5120]{2,1,0:T(8,128)(2,1)}), bf16[16,40,5120]{2,1,0:T(8,128)(2,1)}, u32[]{:S(2)}, u32[]{:S(2)}) async-start(bf16[16,40,5120]{2,1,0:T(8,128)(2,1)} %bitcast.33), calls=%async_computation.3 | async-start | bytes 13107200 | tf_op jit(solution)/shard_map/all_to_all | solution.py:508
